TPU v7x, 32 devices: a whole 2x2x4 slice. The times are simulated.
32 devices in a mesh: gx: 8 (over z, core), gy: 4 (over y, x).
Axes of the slice: x: 2, y: 2, z: 4, core: 2. Of those that a mesh axis runs over, the one named last changes fastest.
Arguments:
- velocity: float32 [3, 2048, 512], P(None, 'gx', 'gy'), may hold values from 0.4 to 1.6
- adjoint_seed: float32 [3, 2048, 512], P(None, 'gx', 'gy'), may hold values from -6 to 6
- courant: float32 [3, 2048, 512], P(None, 'gx', 'gy'), may hold values from 0.1 to 0.45
- viscosity: float32 [3, 2048, 512], P(None, 'gx', 'gy'), may hold values from 0.02 to 0.1
- turbine_tile: int32 [128, 1], P(('gx', 'gy')), may hold values from 0 to 31; in each aligned block of 128 rows (0 to 127, 128 to 255, ...) at most 12 rows name the same one
- turbine_offset: int32 [128, 2], P(('gx', 'gy')), may hold values from 0 to 64
- thrust: float32 [128], P(('gx', 'gy')), may hold values from 0.5 to 2
- disk_width: float32 [128], P(('gx', 'gy')), may hold values from 8 to 16
Outputs:
- adjoint_start: float32 [3, 2048, 512], P(None, 'gx', 'gy')
- thrust_grad: float32 [128], P(('gx', 'gy'))
Inputs may be any that keep to these rules, and one draw needn't show every extreme that they name: `turbine_tile`: each turbine's tile is the index along gx times the number of devices of gy plus the index along gy of the device whose cells hold its footprint. No tile holds more than 12 turbines, and some tile holds exactly 12.
All inputs are finite; a program needn't handle non-finite values.
Results may differ from a plain program's by a relative error of at most 0.00002.
Values sent between devices are 32-bit elements; how exact they have to be, the bound alone decides.
No kernel may reach another device: no remote copies, remote signals or barrier semaphores. Data moves between devices by JAX's collectives and lax.ppermute only.
A program may use at most 128 MiB of HBM per device.

v0:
```python
import jax
import jax.numpy as jnp
from jax import lax
from jax.sharding import PartitionSpec as P

LEV = 3
STEPS = 8
FP = 64


VERTICAL_MIX = 0.05
DRAG_SCALE = 0.01


def padded_2(block, sides, width):
    for axis, dim in sides:
        count = lax.axis_size(axis)
        forward = [(i, i + 1) for i in range(count - 1)]
        forward.append((count - 1, 0))
        backward = [(target, source) for source, target in forward]
        low = lax.ppermute(
            lax.slice_in_dim(block, block.shape[dim] - width, None, axis=dim), axis, forward
        )
        high = lax.ppermute(lax.slice_in_dim(block, 0, width, axis=dim), axis, backward)
        block = jnp.concatenate([low, block, high], axis=dim)
    return block


def drag_law(state):
    return state * jnp.sqrt(state * state + 1.0)


def drag_slope(state):
    square_one = state * state + 1.0
    return (square_one + state * state) / jnp.sqrt(square_one)


def vertical(center):
    zero_row = jnp.zeros_like(center[:1])
    from_above = jnp.concatenate([center[1:] - center[:-1], zero_row], axis=0)
    from_below = jnp.concatenate([zero_row, center[:-1] - center[1:]], axis=0)
    return from_above + from_below


def advance(padded, advect, diffuse, drag_coef):
    center = padded[:, 1:-1, 1:-1]
    upwind = padded[:, :-2, 1:-1]
    downwind = padded[:, 2:, 1:-1]
    left_cell = padded[:, 1:-1, :-2]
    right_cell = padded[:, 1:-1, 2:]
    return (
        center
        + advect * (upwind - center)
        + diffuse * (downwind + upwind + right_cell + left_cell - 4.0 * center)
        + VERTICAL_MIX * vertical(center)
        - drag_coef * drag_law(center)
    )


def retreat(padded, advect_ext, diffuse_ext, drag_coef, state):
    flux_adv = advect_ext * padded
    flux_dif = diffuse_ext * padded
    center = padded[:, 1:-1, 1:-1]
    return (
        center
        - flux_adv[:, 1:-1, 1:-1]
        - 4.0 * flux_dif[:, 1:-1, 1:-1]
        + flux_adv[:, 2:, 1:-1]
        + (
            flux_dif[:, 2:, 1:-1]
            + flux_dif[:, :-2, 1:-1]
            + flux_dif[:, 1:-1, 2:]
            + flux_dif[:, 1:-1, :-2]
        )
        + VERTICAL_MIX * vertical(center)
        - drag_coef * drag_slope(state) * center
    )


def footprint(disk_width):
    cell_pos = jnp.arange(FP, dtype=jnp.float32) - (FP - 1) / 2.0
    profile = jnp.exp(
        -(cell_pos[None, :] * cell_pos[None, :]) / (2.0 * disk_width[:, None] * disk_width[:, None])
    )
    level_pos = jnp.arange(LEV, dtype=jnp.float32) - (LEV - 1) / 2.0
    level_gain = DRAG_SCALE * jnp.exp(-0.5 * level_pos * level_pos)
    return level_gain[None, :, None, None] * profile[:, None, :, None] * profile[:, None, None, :]


def extend_rim(array, rim_depth):
    return padded_2(array, (("gx", 1), ("gy", 2)), rim_depth)


def trim_rim(array, stored_margin, wanted):
    excess = stored_margin - wanted
    if excess == 0:
        return array
    return array[:, excess:-excess, excess:-excess]


def coef_at(coef_ext, coef_margin, wanted, levels):
    portion = trim_rim(coef_ext, coef_margin, wanted)
    return (portion[:levels], portion[levels : 2 * levels], portion[2 * levels : 3 * levels])


def shards(
    velocity, adjoint_seed, courant, viscosity, turbine_tile, turbine_offset, thrust, disk_width
):
    levels = velocity.shape[0]
    places, shifts = (
        lax.all_gather(turbine_tile, ("gx", "gy"), axis=0, tiled=True),
        lax.all_gather(turbine_offset, ("gx", "gy"), axis=0, tiled=True),
    )
    thrusts, widths = (
        lax.all_gather(thrust, ("gx", "gy"), axis=0, tiled=True),
        lax.all_gather(disk_width, ("gx", "gy"), axis=0, tiled=True),
    )
    turbine_count = places.shape[0]
    own_index = lax.axis_index("gx") * lax.axis_size("gy") + lax.axis_index("gy")
    turbine_ids = jnp.arange(turbine_count, dtype=jnp.int32)
    in_tile = places[:, 0] == own_index
    sort_keys = jnp.where(in_tile, turbine_ids, turbine_ids + turbine_count)
    slot_count = 3 * thrust.shape[0]
    slot_ids = jnp.argsort(sort_keys)[:slot_count]
    slot_match = in_tile[slot_ids]
    slot_live = slot_match.astype(jnp.float32)
    slot_rows = shifts[slot_ids, 0]
    slot_cols = shifts[slot_ids, 1]
    kernels = footprint(widths[slot_ids])
    slot_thrust = thrusts[slot_ids] * slot_live

    def add_turbine(slot_index, field_now):
        corner = (jnp.int32(0), slot_rows[slot_index], slot_cols[slot_index])
        block_vals = lax.dynamic_slice(field_now, corner, (levels, FP, FP))
        return lax.dynamic_update_slice(
            field_now, block_vals + slot_thrust[slot_index] * kernels[slot_index], corner
        )

    drag_field = lax.fori_loop(0, slot_count, add_turbine, jnp.zeros_like(velocity))
    forward_depth = 1
    coef_margin = 1
    coef_margin = forward_depth
    coef_ext = extend_rim(jnp.concatenate([courant, viscosity, drag_field], axis=0), forward_depth)
    state = velocity
    state_margin = 0
    states = []
    for step_index in range(STEPS):
        if step_index + 1 < STEPS and state_margin == 0:
            state = extend_rim(state, forward_depth)
            state_margin = forward_depth
        states.append((state, state_margin))
        if step_index + 1 < STEPS:
            advect, diffuse, drag_coef = coef_at(coef_ext, coef_margin, state_margin - 1, levels)
            state = advance(state, advect, diffuse, drag_coef)
            state_margin = state_margin - 1
    adjoint = adjoint_seed
    adjoint_margin = 0
    sensitivity = jnp.zeros_like(velocity)
    for step_index in reversed(range(STEPS)):
        stored, stored_margin = states[step_index]
        sensitivity = sensitivity - trim_rim(adjoint, adjoint_margin, 0) * drag_law(
            trim_rim(stored, stored_margin, 0)
        )
        adjoint = extend_rim(adjoint, forward_depth)
        adjoint_margin = forward_depth
        advect_ext, diffuse_ext, unused_drag = coef_at(
            coef_ext, coef_margin, adjoint_margin, levels
        )
        unused_adv, unused_dif, drag_mid = coef_at(
            coef_ext, coef_margin, adjoint_margin - 1, levels
        )
        adjoint = retreat(
            adjoint,
            advect_ext,
            diffuse_ext,
            drag_mid,
            trim_rim(stored, stored_margin, adjoint_margin - 1),
        )
        adjoint_margin = adjoint_margin - 1
    adjoint_start = trim_rim(adjoint, adjoint_margin, 0)

    def slot_total(row_first, col_first, kernel):
        block_vals = lax.dynamic_slice(
            sensitivity, (jnp.int32(0), row_first, col_first), (levels, FP, FP)
        )
        return jnp.sum(kernel * block_vals)

    totals = jax.vmap(slot_total)(slot_rows, slot_cols, kernels)
    values = thrusts[slot_ids] * totals * slot_live
    one_hot = (turbine_ids[None, :] == slot_ids[:, None]).astype(jnp.float32)
    spread = jnp.sum(one_hot * values[:, None], axis=0)
    return (adjoint_start, lax.psum_scatter(spread, ("gx", "gy"), scatter_dimension=0, tiled=True))


def solution(mesh):
    placed = (
        P(None, "gx", "gy"),
        P(None, "gx", "gy"),
        P(None, "gx", "gy"),
        P(None, "gx", "gy"),
        P(("gx", "gy"), None),
        P(("gx", "gy"), None),
        P(("gx", "gy")),
        P(("gx", "gy")),
    )
    return jax.shard_map(
        shards,
        mesh=mesh,
        in_specs=placed,
        out_specs=(P(None, "gx", "gy"), P(("gx", "gy"))),
        check_vma=False,
    )
```

profile of v0, /device:TPU:0, one launch (start us, length us, event | category | flops | bytes accessed | tf_op | source)
XLA Modules:
  0.0 685.8 jit_solution(3933051463795110994)
XLA Ops:
  1.4 4.5 collective-permute-start.9
  7.9 38.9 %all-reduce.32 = s32[128]{0:T(128)S(1)} all-reduce(s32[128]{0:T(128)S(1)} %bitcast_dynamic-update-slice_fusion.1), channel_id=1, replica_groups=mesh['gx'=8,'gy'=4] {'gx','gy'}, use_global_device_ids=true, to_apply=%add.32 | all-reduce | flops 128 | bytes 1024
  46.8 2.6 sort.17
  50.0 65.9 %all-gather = s32[32,4,2]{1,2,0:T(2,128)S(1)} all-gather(s32[1,4,2]{1,2,0:T(2,128)} %bitcast.32), channel_id=1, replica_groups=mesh['gx'=8,'gy'=4] {'gx','gy'}, dimensions={0}, use_global_device_ids=true | all-gather | bytes 1056 | tf_op jit(solution)/shard_map/all_gather | solution.py:112
  118.6 36.9 %all-reduce.36 = (f32[128]{0:T(128)S(1)}, f32[128]{0:T(128)S(1)}) all-reduce(f32[128]{0:T(128)S(1)} %dynamic-update-slice.3, f32[128]{0:T(128)S(1)} %dynamic-update-slice.4), channel_id=1, replica_groups=mesh['gx'=8,'gy'=4] {'gx','gy'}, use_global_device_ids=true, to_apply=%add.33 | all-reduce | flops 256 | bytes 2048
  157.7 99.8 %while.14 = (s32[]{:T(128)}, f32[3,256,128]{2,1,0:T(8,128)S(1)}, s32[12]{0:T(128)S(1)}, s32[12]{0:T(128)S(1)}, f32[12]{0:T(128)S(1)}, /*index=5*/f32[12,3,64,64]...) while((s32[]{:T(128)}, f32[3,256,128]{2,1,0:T(8,128)S(1)}, s32[12]{0:T(128)S(1)}, ...), condition=%wide.region_2.3_spmd, body=%wide.region_1.2_spmd.sunk | while | flops 24584 | bytes 245993 | solution.py:139
  265.3 3.4 fusion.4
  270.1 3.6 collective-permute-done.12
  274.5 2.4 collective-permute-start.15
  282.1 6.0 fusion.113
  288.7 3.1 collective-permute-start.5
  301.7 5.9 fusion.102
  307.6 2.5 collective-permute-start.21
  311.4 3.5 collective-permute-done.20
  324.5 5.9 fusion.91
  331.4 2.1 collective-permute-start.7
  344.4 6.0 fusion.80
  363.7 5.0 fusion.69
  370.5 3.6 collective-permute-start.1
  384.2 2.7 fusion.150
  386.9 2.6 copy.630
  390.2 2.6 copy.629
  399.1 2.6 copy.632
  401.7 2.6 copy.631
  404.3 5.1 fusion.131
  409.6 4.9 fusion.130
  414.6 4.1 fusion.121
  421.4 3.5 collective-permute-done.36
  432.9 2.3 slice_subtract_fusion.21
  439.1 2.5 fusion.147
  444.7 3.6 collective-permute-done.40
  456.2 2.2 slice_subtract_fusion.19
  462.9 2.5 fusion.145
  468.5 3.6 collective-permute-done.44
  480.1 2.3 slice_subtract_fusion.17
  486.8 2.5 fusion.143
  492.4 3.6 collective-permute-done.48
  499.8 2.1 collective-permute-start.51
  503.9 2.3 slice_subtract_fusion.15
  510.5 2.5 fusion.141
  516.1 3.6 collective-permute-done.52
  527.9 2.3 slice_subtract_fusion.13
  534.5 2.5 fusion.139
  541.7 3.6 collective-permute-done.56
  549.7 2.2 collective-permute-start.59
  553.7 2.3 slice_subtract_fusion.11
  560.5 2.5 fusion.137
  563.4 9.2 %multiply_subtract_fusion = (f32[3,256,128]{2,0,1:T(4,128)S(1)}, f32[3,256,128]{2,0,1:T(4,128)S(1)}) fusion(f32[3,256,128]{2,0,1:T(4,128)} %copy-done.40, f32[3,256,128]{2,0,1:T(4,128)S(1)} %copy-done.18, f32[3,256,128]{2,0,1:T(4,128)S(1)} %copy-done.15, f32[3,256,128]{2,0,1:T(4,128)S(1)} %copy-done.12, f32[3,256,128]{2,0,1:T(4,128)S(1)} %copy-done.9, ...), kind=kLoop, calls=%fused_computation.278 | loop fusion | flops 7766016 | bytes 11281456 | tf_op jit(solution)/shard_map/sub | solution.py:161
  575.0 49.5 %while.15 = (s32[]{:T(128)}, f32[3,256,128]{2,1,0:T(8,128)}, s32[12,3]{0,1:T(4,128)}, f32[12,3,64,64]{3,2,1,0:T(8,128)}, s32[]{:T(128)}) while((s32[]{:T(128)}, f32[3,256,128]{2,1,0:T(8,128)}, s32[12,3]{0,1:T(4,128)}, f32[12,3,64,64]{3,2,1,0:T(8,128)}, s32[]{:T(128)}) %tuple.129), condition=%wide.while_cond, body=%wide.while_body.sunk | while | flops 2 | bytes 197749 | solution.py:183
  576.3 2.8 bitcast_dynamic-update-slice_fusion.3
  580.4 2.8 bitcast_dynamic-update-slice_fusion.3
  584.5 2.8 bitcast_dynamic-update-slice_fusion.3
  588.6 2.8 bitcast_dynamic-update-slice_fusion.3
  592.8 2.8 bitcast_dynamic-update-slice_fusion.3
  596.9 2.8 bitcast_dynamic-update-slice_fusion.3
  601.0 2.8 bitcast_dynamic-update-slice_fusion.3
  605.1 2.8 bitcast_dynamic-update-slice_fusion.3
  609.3 2.8 bitcast_dynamic-update-slice_fusion.3
  613.4 2.8 bitcast_dynamic-update-slice_fusion.3
  617.5 2.8 bitcast_dynamic-update-slice_fusion.3
  621.6 2.8 bitcast_dynamic-update-slice_fusion.3
  630.8 2.2 collective-permute-start.63
  636.3 39.4 %all-reduce.35 = f32[128]{0:T(128)} all-reduce(f32[128]{0:T(128)} %select_reduce_fusion), channel_id=2, replica_groups=mesh['gx'=8,'gy'=4] {'gx','gy'}, use_global_device_ids=true, to_apply=%region_5.6.clone | all-reduce | flops 128 | bytes 1024
  680.5 2.2 fusion.135
  (570 shorter events, 266.6 us)
Async XLA Ops:
  1.4 257.0 %collective-permute-start.9 = (f32[3,1,128]{2,1,0:T(1,128)S(1)}, f32[3,1,128]{2,1,0:T(1,128)S(1)}, u32[]{:S(2)}, u32[]{:S(2)}) collective-permute-start(f32[3,1,128]{2,1,0:T(1,128)S(1)} %get-tuple-element.326), channel_id=1, source_target_pairs={{4,0},{8,4},{12,8},{16,12},{20,16},{24,20},{28,24},{0,28},{5,1},{9... | collective-permute-start | bytes 4616 | tf_op jit(solution)/shard_map/ppermute | solution.py:24
  5.8 252.6 %collective-permute-start.8 = (f32[3,1,128]{2,1,0:T(1,128)S(1)}, f32[3,1,128]{2,1,0:T(1,128)S(1)}, u32[]{:S(2)}, u32[]{:S(2)}) collective-permute-start(f32[3,1,128]{2,1,0:T(1,128)S(1)} %get-tuple-element.327), channel_id=1, source_target_pairs={{0,4},{4,8},{8,12},{12,16},{16,20},{20,24},{24,28},{28,0},{1,5},{5... | collective-permute-start | bytes 4616 | tf_op jit(solution)/shard_map/ppermute | solution.py:21
  259.0 4.5 collective-permute-start.11
  260.5 3.6 collective-permute-start.10
  268.7 1.4 collective-permute-start.13
  268.8 4.9 collective-permute-start.12
  274.5 4.6 collective-permute-start.15
  277.1 3.8 collective-permute-start.14
  288.1 4.8 collective-permute-start.17
  288.2 4.9 collective-permute-start.16
  288.7 21.4 %collective-permute-start.5 = (f32[3,1,128]{2,1,0:T(1,128)S(1)}, f32[3,1,128]{2,1,0:T(1,128)S(1)}, u32[]{:S(2)}, u32[]{:S(2)}) collective-permute-start(f32[3,1,128]{2,1,0:T(1,128)S(1)} %get-tuple-element.329), channel_id=1, source_target_pairs={{4,0},{8,4},{12,8},{16,12},{20,16},{24,20},{28,24},{0,28},{5,1},{9... | collective-permute-start | bytes 4616 | tf_op jit(solution)/shard_map/ppermute | solution.py:24
  291.9 18.8 %collective-permute-start.4 = (f32[3,1,128]{2,1,0:T(1,128)S(1)}, f32[3,1,128]{2,1,0:T(1,128)}, u32[]{:S(2)}, u32[]{:S(2)}) collective-permute-start(f32[3,1,128]{2,1,0:T(1,128)S(1)} %get-tuple-element.328), channel_id=1, source_target_pairs={{0,4},{4,8},{8,12},{12,16},{16,20},{20,24},{24,28},{28,0},{1,5},{5... | collective-permute-start | bytes 4616 | tf_op jit(solution)/shard_map/ppermute | solution.py:21
  295.6 4.5 collective-permute-start.19
  296.9 3.7 collective-permute-start.18
  307.6 3.8 collective-permute-start.21
  310.1 4.8 collective-permute-start.20
  317.5 4.5 collective-permute-start.23
  319.5 3.9 collective-permute-start.22
  330.4 3.4 collective-permute-start.25
  330.5 4.9 collective-permute-start.24
  331.4 21.5 %collective-permute-start.7 = (f32[3,258,1]{1,0,2:T(4,128)S(1)}, f32[3,258,1]{1,0,2:T(4,128)S(1)}, u32[]{:S(2)}, u32[]{:S(2)}) collective-permute-start(f32[3,258,1]{1,0,2:T(4,128)S(1)} %copy.743), channel_id=1, source_target_pairs={{1,0},{2,1},{3,2},{0,3},{5,4},{6,5},{7,6},{4,7},{9,8},{10,9},{11,1... | collective-permute-start | bytes 9296 | tf_op jit(solution)/shard_map/ppermute | solution.py:24
  333.8 20.2 %collective-permute-start.6 = (f32[3,258,1]{1,0,2:T(4,128)S(1)}, f32[3,258,1]{1,0,2:T(4,128)S(1)}, u32[]{:S(2)}, u32[]{:S(2)}) collective-permute-start(f32[3,258,1]{1,0,2:T(4,128)S(1)} %copy.742), channel_id=1, source_target_pairs={{0,1},{1,2},{2,3},{3,0},{4,5},{5,6},{6,7},{7,4},{8,9},{9,10},{10,1... | collective-permute-start | bytes 9296 | tf_op jit(solution)/shard_map/ppermute | solution.py:21
  337.9 4.5 collective-permute-start.27
  339.6 3.7 collective-permute-start.26
  350.4 4.8 collective-permute-start.29
  350.9 4.8 collective-permute-start.28
  356.5 4.6 collective-permute-start.31
  358.6 3.9 collective-permute-start.30
  368.7 5.4 collective-permute-start.33
  370.5 4.8 collective-permute-start.32
  370.5 13.0 %collective-permute-start.1 = (f32[9,1,128]{2,0,1:T(8,128)S(1)}, f32[9,1,128]{2,0,1:T(8,128)S(1)}, u32[]{:S(2)}, u32[]{:S(2)}) collective-permute-start(f32[9,1,128]{2,0,1:T(8,128)S(1)} %get-tuple-element.233), channel_id=1, source_target_pairs={{4,0},{8,4},{12,8},{16,12},{20,16},{24,20},{28,24},{0,28},{5,1},{9... | collective-permute-start | bytes 13832 | tf_op jit(solution)/shard_map/ppermute | solution.py:24
  374.1 9.4 %collective-permute-start = (f32[9,1,128]{2,0,1:T(8,128)S(1)}, f32[9,1,128]{2,0,1:T(8,128)S(1)}, u32[]{:S(2)}, u32[]{:S(2)}) collective-permute-start(f32[9,1,128]{2,0,1:T(8,128)S(1)} %get-tuple-element.232), channel_id=1, source_target_pairs={{0,4},{4,8},{8,12},{12,16},{16,20},{20,24},{24,28},{28,0},{1,5},{5... | collective-permute-start | bytes 13832 | tf_op jit(solution)/shard_map/ppermute | solution.py:21
  378.7 16.8 %collective-permute-start.35 = (f32[3,258,1]{1,0,2:T(4,128)S(1)}, f32[3,258,1]{1,0,2:T(4,128)}, u32[]{:S(2)}, u32[]{:S(2)}) collective-permute-start(f32[3,258,1]{1,0,2:T(4,128)S(1)} %copy.698), channel_id=1, source_target_pairs={{0,1},{1,2},{2,3},{3,0},{4,5},{5,6},{6,7},{7,4},{8,9},{9,10},{10,1... | collective-permute-start | bytes 9296 | tf_op jit(solution)/shard_map/ppermute | solution.py:21
  382.1 15.1 %collective-permute-start.34 = (f32[3,258,1]{1,0,2:T(4,128)}, f32[3,258,1]{1,0,2:T(4,128)}, u32[]{:S(2)}, u32[]{:S(2)}) collective-permute-start(f32[3,258,1]{1,0,2:T(4,128)} %copy.696), channel_id=1, source_target_pairs={{1,0},{2,1},{3,2},{0,3},{5,4},{6,5},{7,6},{4,7},{9,8},{10,9},{11,1... | collective-permute-start | bytes 9296 | tf_op jit(solution)/shard_map/ppermute | solution.py:24
  389.5 9.6 %collective-permute-start.3 = (f32[9,258,1]{1,0,2:T(8,128)S(1)}, f32[9,258,1]{1,0,2:T(8,128)S(1)}, u32[]{:S(2)}, u32[]{:S(2)}) collective-permute-start(f32[9,258,1]{1,0,2:T(8,128)S(1)} %copy.630), channel_id=1, source_target_pairs={{1,0},{2,1},{3,2},{0,3},{5,4},{6,5},{7,6},{4,7},{9,8},{10,9},{11,1... | collective-permute-start | bytes 27872 | tf_op jit(solution)/shard_map/ppermute | solution.py:24
  392.8 8.8 %collective-permute-start.2 = (f32[9,258,1]{1,0,2:T(8,128)S(1)}, f32[9,258,1]{1,0,2:T(8,128)S(1)}, u32[]{:S(2)}, u32[]{:S(2)}) collective-permute-start(f32[9,258,1]{1,0,2:T(8,128)S(1)} %copy.629), channel_id=1, source_target_pairs={{0,1},{1,2},{2,3},{3,0},{4,5},{5,6},{6,7},{7,4},{8,9},{9,10},{10,1... | collective-permute-start | bytes 27872 | tf_op jit(solution)/shard_map/ppermute | solution.py:21
  418.8 2.6 collective-permute-start.37
  420.1 4.8 collective-permute-start.36
  428.8 6.3 collective-permute-start.39
  432.3 5.0 collective-permute-start.38
  443.4 1.4 collective-permute-start.41
  443.4 4.9 collective-permute-start.40
  452.2 6.3 collective-permute-start.43
  456.2 4.8 collective-permute-start.42
  467.1 1.4 collective-permute-start.45
  467.2 4.9 collective-permute-start.44
  475.9 6.5 collective-permute-start.47
  479.9 5.0 collective-permute-start.46
  491.0 1.4 collective-permute-start.49
  491.1 4.9 collective-permute-start.48
  499.8 6.3 collective-permute-start.51
  503.9 4.8 collective-permute-start.50
  514.8 1.4 collective-permute-start.53
  514.8 4.9 collective-permute-start.52
  523.6 6.6 collective-permute-start.55
  527.6 5.1 collective-permute-start.54
  540.1 1.5 collective-permute-start.57
  540.1 5.1 collective-permute-start.56
  549.7 6.4 collective-permute-start.59
  553.7 4.8 collective-permute-start.58
  573.6 53.2 %collective-permute-start.61 = (f32[3,1,128]{2,0,1:T(4,128)}, f32[3,1,128]{2,0,1:T(4,128)}, u32[]{:S(2)}, u32[]{:S(2)}) collective-permute-start(f32[3,1,128]{2,0,1:T(4,128)} %get-tuple-element.263), channel_id=1, source_target_pairs={{4,0},{8,4},{12,8},{16,12},{20,16},{24,20},{28,24},{0,28},{5,1},{9... | collective-permute-start | bytes 4616 | tf_op jit(solution)/shard_map/ppermute | solution.py:24
  573.7 53.1 %collective-permute-start.60 = (f32[3,1,128]{2,0,1:T(4,128)}, f32[3,1,128]{2,0,1:T(4,128)}, u32[]{:S(2)}, u32[]{:S(2)}) collective-permute-start(f32[3,1,128]{2,0,1:T(4,128)} %get-tuple-element.262), channel_id=1, source_target_pairs={{0,4},{4,8},{8,12},{12,16},{16,20},{20,24},{24,28},{28,0},{1,5},{5... | collective-permute-start | bytes 4616 | tf_op jit(solution)/shard_map/ppermute | solution.py:21
  630.8 46.1 %collective-permute-start.63 = (f32[3,258,1]{1,0,2:T(4,128)}, f32[3,258,1]{1,0,2:T(4,128)}, u32[]{:S(2)}, u32[]{:S(2)}) collective-permute-start(f32[3,258,1]{1,0,2:T(4,128)} %copy.735), channel_id=1, source_target_pairs={{1,0},{2,1},{3,2},{0,3},{5,4},{6,5},{7,6},{4,7},{9,8},{10,9},{11,1... | collective-permute-start | bytes 9296 | tf_op jit(solution)/shard_map/ppermute | solution.py:24
  635.0 43.8 %collective-permute-start.62 = (f32[3,258,1]{1,0,2:T(4,128)}, f32[3,258,1]{1,0,2:T(4,128)}, u32[]{:S(2)}, u32[]{:S(2)}) collective-permute-start(f32[3,258,1]{1,0,2:T(4,128)} %copy.734), channel_id=1, source_target_pairs={{0,1},{1,2},{2,3},{3,0},{4,5},{5,6},{6,7},{7,4},{8,9},{9,10},{10,1... | collective-permute-start | bytes 9296 | tf_op jit(solution)/shard_map/ppermute | solution.py:21
  (106 other events, 801.7 us)
where the time goes:
time: 697 us; the launch traced here: 686 us
  local copies, waits for them, and re-layouts  218 us (31%)
  blocking collectives  181 us (26%)
  other arithmetic  127 us (18%)
  starting transfers between devices  64 us (9%)
  waiting for transfers between devices  46.8 us (7%)
  loops' own time  46.2 us (7%)
    unnamed x3, blocking collectives  115 us
    all_gather x1, blocking collectives, shards(): lax.all_gather(turbine_offset, ('gx', 'gy'), axis=0, tiled=True)  65.9 us
    gather x36, local copies, waits for them, and re-layouts  49.5 us
    another operation x1, loops' own time, shards(): lax.fori_loop(0, slot_count, add_turbine, jnp.zeros_like(velocity))  46.2 us
    ppermute x32, starting transfers between devices, padded_2(): lax.ppermute(lax.slice_in_dim(block, 0, width, axis=dim), axis, backward)  45.5 us
    ppermute x32, waiting for transfers between devices, padded_2(): lax.ppermute(lax.slice_in_dim(block, block.shape[dim] - width, None, axis...  37.6 us
    slice x37, local copies, waits for them, and re-layouts, padded_2(): lax.slice_in_dim(block, block.shape[dim] - width, None, axis=dim)  34.9 us
    sub x6, other arithmetic, advance(): center + advect * (upwind - center)  32.3 us
  transfers between devices with their start and end apart: 64, of which 36 were waited for; matrix products, arithmetic and copies ran while one was open for 31% of the time, Pallas kernels for 0%

commit v1 on v0

v1 whole, which is shorter than its diff:
```python
import functools
import math

import jax
import jax.numpy as jnp
from jax import lax
from jax.experimental import pallas as pl
from jax.experimental.pallas import tpu as pltpu
from jax.sharding import PartitionSpec as P

STEPS = 8
FP = 64
VERTICAL_MIX = 0.05
DRAG_SCALE = 0.01
SIDE_GAIN = math.exp(-0.5)

LEV, CX, CY = 3, 256, 128
WIDE = 14
MID = 13
THIN = 8
GAP = 42
RIM = 16
TOP = 24
TALL = CX + 2 * TOP
SIDE_ROWS = CX + 64
END_ROWS = 3 * LEV * RIM + LEV * THIN + 2 * RIM + 2 * THIN
VALUES = 6
FORWARD_ROWS = 32
ADJOINT_ROWS = 32


def lane_ids():
    return lax.broadcasted_iota(jnp.int32, (1, CY), 1)


def spread_lanes(value, rows):
    return jnp.broadcast_to(value, (rows, CY))


def rolled(value, shift):
    shift = shift % CY
    return value if shift == 0 else pltpu.roll(value, shift, 1)


def rim_place(lane):
    level = jnp.where((lane >= GAP // 2) & (lane < GAP // 2 + GAP), 1, 0)
    level = jnp.where((lane >= GAP // 2 + GAP) & (lane < GAP // 2 + 2 * GAP), 2, level)
    place = lane - GAP * level
    place = jnp.where(lane >= GAP // 2 + 2 * GAP, lane - CY, place)
    return level, place


def for_rows(first, count, chunk, body):
    full = count // chunk
    if full == 1:
        body(first, chunk)
    elif full > 1:

        def one(index, carry):
            body(pl.multiple_of(first + index * chunk, 8), chunk)
            return carry

        lax.fori_loop(0, full, one, 0)
    if count > full * chunk:
        body(first + full * chunk, count - full * chunk)


def pack_sides(
    n_gy, tile_ref, offset_ref, thrust_ref, width_ref, vel_ref, seed_ref, cou_ref, vis_ref,
    up_ref, down_ref, info_ref,
):
    lane = lane_ids()
    whole = jnp.zeros((1, CY), jnp.int32)
    real = jnp.zeros((1, CY), jnp.float32)
    for k in range(thrust_ref.shape[0]):
        tile = tile_ref[k, 0]
        for spot, value in enumerate(
            (tile // n_gy, tile % n_gy, offset_ref[k, 0], offset_ref[k, 1])
        ):
            whole = jnp.where(lane == VALUES * k + spot, value, whole)
        real = jnp.where(lane == VALUES * k + 4, thrust_ref[k], real)
        real = jnp.where(lane == VALUES * k + 5, width_ref[k], real)
    info_ref[...] = jnp.broadcast_to(whole.astype(jnp.float32) + real, info_ref.shape)

    for out_ref, low in ((up_ref, False), (down_ref, True)):

        def one(first, rows, out_ref=out_ref, low=low):
            total = jnp.zeros((rows, CY), jnp.float32)
            start = 0
            for ref, width in ((vel_ref, WIDE), (cou_ref, MID), (vis_ref, MID)):
                for level in range(LEV):
                    to = GAP * level + start
                    moved = rolled(
                        ref[level, pl.ds(first, rows), :], to - (0 if low else CY - width)
                    )
                    total = jnp.where((lane >= to) & (lane < to + width), moved, total)
                start += width
            out_ref[pl.ds(first, rows), :] = total

        for_rows(0, CX, 32, one)
        total = jnp.zeros((64, CY), jnp.float32)
        for block in range(4):
            for level in range(LEV):
                to = 32 * block + THIN * level
                moved = rolled(
                    seed_ref[level, 64 * block : 64 * block + 64, :],
                    to - (0 if low else CY - THIN),
                )
                total = jnp.where((lane >= to) & (lane < to + THIN), moved, total)
        out_ref[CX:SIDE_ROWS, :] = total


def pack_ends(west_ref, east_ref, vel_ref, seed_ref, cou_ref, vis_ref, up_ref, down_ref):
    for out_ref, low in ((up_ref, False), (down_ref, True)):
        at = 0
        first = 0 if low else CX - RIM
        for ref in (vel_ref, cou_ref, vis_ref):
            for level in range(LEV):
                out_ref[at : at + RIM, :] = ref[level, first : first + RIM, :]
                at += RIM
        thin_first = 0 if low else CX - THIN
        for level in range(LEV):
            out_ref[at : at + THIN, :] = seed_ref[level, thin_first : thin_first + THIN, :]
            at += THIN
        for ref in (west_ref, east_ref):
            out_ref[at : at + RIM, :] = ref[first : first + RIM, :]
            at += RIM
        side_first = CX if low else SIDE_ROWS - THIN
        for ref in (west_ref, east_ref):
            out_ref[at : at + THIN, :] = ref[side_first : side_first + THIN, :]
            at += THIN


def window(
    n_gx, n_gy, per_device,
    place_ref, info_ref, vel_ref, seed_ref, cou_ref, vis_ref, west_ref, east_ref, low_ref, high_ref,
    start_ref, grads_ref,
    u_buf, l_buf, g_buf, f_buf, a_buf, w_buf, v_buf, d_buf, s_buf, rows_buf, cols_buf,
):
    lane = lane_ids()
    level_of, place = rim_place(lane)
    west_lane, east_lane = place == -1, place == 0
    level_one, level_two = level_of == 1, level_of == 2
    valid = (place >= -WIDE) & (place < WIDE)
    from_above = jnp.where(valid & (level_of < LEV - 1), VERTICAL_MIX, 0.0).astype(jnp.float32)
    from_below = jnp.where(valid & (level_of > 0), VERTICAL_MIX, 0.0).astype(jnp.float32)
    rim_mix = from_above + from_below
    first_lane, last_lane = lane == 0, lane == CY - 1

    devices = info_ref.shape[0]
    my_gx = place_ref[0].astype(jnp.float32)
    my_gy = place_ref[1].astype(jnp.float32)
    col_of = jnp.where(place < 0, place, CY + place).astype(jnp.float32)
    row_lane = lax.broadcasted_iota(jnp.int32, (1, 3 * CY), 1).astype(jnp.float32)
    row_profiles, rim_profiles = [], []

    def near(delta, count):
        delta = jnp.where(delta >= count / 2, delta - count, delta)
        return jnp.where(delta < -count / 2, delta + count, delta)

    def profile(cells, first, width):
        at = cells - first
        centred = at - (FP - 1) / 2.0
        value = jnp.exp(-(centred * centred) / (2.0 * width * width))
        return jnp.where((at >= 0.0) & (at < float(FP)), value, 0.0)

    for k in range(per_device):
        info = info_ref[:, VALUES * k : VALUES * k + VALUES]
        row_first = near(info[:, 0:1] - my_gx, n_gx) * CX + info[:, 2:3]
        col_first = near(info[:, 1:2] - my_gy, n_gy) * CY + info[:, 3:4]
        scale = DRAG_SCALE * info[:, 4:5]
        width = info[:, 5:6]
        part = pl.ds(k * devices, devices)
        row_profiles.append(profile(row_lane - RIM, row_first, width) * scale)
        rows_buf[part, :] = profile(row_lane[:, :CX], row_first, width) * scale
        cols_buf[part, :] = profile(lane.astype(jnp.float32), col_first, width)
        rim_profiles.append(profile(col_of, col_first, width))
    along_rows = jnp.concatenate(row_profiles, axis=0)
    along_cols = jnp.concatenate([cols_buf[...], jnp.concatenate(rim_profiles, axis=0)], axis=1)
    drag = lax.dot_general(
        along_rows.T, along_cols, (((1,), (0,)), ((), ())),
        precision=lax.Precision.HIGHEST, preferred_element_type=jnp.float32,
    )
    tall = pl.ds(TOP - RIM, CX + 2 * RIM)
    gain = jnp.where(valid, jnp.where(level_one, 1.0, SIDE_GAIN), 0.0).astype(jnp.float32)
    d_buf[0, tall, :] = drag[: CX + 2 * RIM, :CY]
    d_buf[1, tall, :] = drag[: CX + 2 * RIM, :CY] * SIDE_GAIN
    d_buf[2, tall, :] = drag[: CX + 2 * RIM, CY:] * gain

    edge = jnp.zeros((TOP - RIM, CY), jnp.float32)
    for tile in range(LEV + 1):
        for buf in (a_buf, w_buf, v_buf):
            buf[tile, 0 : TOP - RIM, :] = edge
            buf[tile, TALL - TOP + RIM :, :] = edge
        for buf in (u_buf, l_buf):
            for slot in range(2):
                buf[slot, tile, 0 : TOP - RIM, :] = edge
                buf[slot, tile, TALL - TOP + RIM :, :] = edge
        for slot in range(2):
            l_buf[slot, tile, TOP - RIM : TOP - THIN, :] = edge
            l_buf[slot, tile, TOP + CX + THIN : TOP + CX + RIM, :] = edge

    def coefficients(tile, to, rows, courant, viscosity, mix):
        a_buf[tile, pl.ds(to, rows), :] = 1.0 - courant - 4.0 * viscosity - mix
        w_buf[tile, pl.ds(to, rows), :] = courant + viscosity
        v_buf[tile, pl.ds(to, rows), :] = viscosity

    def level_mix(level):
        return VERTICAL_MIX * (2 if level == 1 else 1)

    def rim(west, east, to, rows):
        zero = jnp.zeros((rows, CY), jnp.float32)
        start = 0
        found = []
        for width in (WIDE, MID, MID):
            value = jnp.where((place >= 0) & (place < width), rolled(east, -start), zero)
            found.append(
                jnp.where((place >= -width) & (place < 0), rolled(west, -start - width), value)
            )
            start += width
        u_buf[0, LEV, pl.ds(to, rows), :] = found[0]
        coefficients(LEV, to, rows, found[1], found[2], rim_mix)

    def thin_rim(west, east, block, to, rows):
        value = jnp.zeros((rows, CY), jnp.float32)
        for level in range(LEV):
            at = GAP * level - (32 * block + THIN * level)
            mine = level_of == level
            value = jnp.where(mine & (place >= 0) & (place < THIN), rolled(east, at), value)
            value = jnp.where(mine & (place >= -THIN) & (place < 0), rolled(west, at - THIN), value)
        l_buf[0, LEV, pl.ds(to, rows), :] = value

    def load_core(first, rows):
        for level in range(LEV):
            at = pl.ds(first, rows)
            u_buf[0, level, pl.ds(first + TOP, rows), :] = vel_ref[level, at, :]
            l_buf[0, level, pl.ds(first + TOP, rows), :] = seed_ref[level, at, :]
            coefficients(
                level, first + TOP, rows, cou_ref[level, at, :], vis_ref[level, at, :], level_mix(level)
            )
        rim(west_ref[pl.ds(first, rows), :], east_ref[pl.ds(first, rows), :], first + TOP, rows)

    for_rows(0, CX, 32, load_core)
    for block in range(4):
        at = pl.ds(CX, 64)
        thin_rim(west_ref[at, :], east_ref[at, :], block, TOP + 64 * block, 64)
    for ref, to, thin_to, block in (
        (low_ref, TOP - RIM, TOP - THIN, 3),
        (high_ref, TOP + CX, TOP + CX, 0),
    ):
        for level in range(LEV):
            u_buf[0, level, to : to + RIM, :] = ref[RIM * level : RIM * level + RIM, :]
            courant = ref[RIM * (LEV + level) : RIM * (LEV + level) + RIM, :]
            viscosity = ref[RIM * (2 * LEV + level) : RIM * (2 * LEV + level) + RIM, :]
            coefficients(level, to, RIM, courant, viscosity, level_mix(level))
            at = 3 * LEV * RIM + THIN * level
            l_buf[0, level, thin_to : thin_to + THIN, :] = ref[at : at + THIN, :]
        at = 3 * LEV * RIM + LEV * THIN
        rim(ref[at : at + RIM, :], ref[at + RIM : at + 2 * RIM, :], to, RIM)
        at += 2 * RIM
        thin_rim(ref[at : at + THIN, :], ref[at + THIN : at + 2 * THIN, :], block, thin_to, THIN)

    def sideways(core, packed):
        sums = []
        for level in range(LEV):
            other = rolled(packed, -GAP * level)
            left = rolled(jnp.where(last_lane, other, core[level]), 1)
            right = rolled(jnp.where(first_lane, other, core[level]), -1)
            sums.append(left + right)
        other = jnp.where(level_one, rolled(core[1], GAP), core[0])
        other = jnp.where(level_two, rolled(core[2], 2 * GAP), other)
        left = rolled(jnp.where(west_lane, other, packed), 1)
        right = rolled(jnp.where(east_lane, other, packed), -1)
        sums.append(left + right)
        return sums

    def upright(core, packed):
        middle = VERTICAL_MIX * core[1]
        mixed = [middle, VERTICAL_MIX * (core[0] + core[2]), middle]
        if packed is not None:
            mixed.append(from_above * rolled(packed, -GAP) + from_below * rolled(packed, GAP))
        return mixed

    def drag_of(tile, at):
        return d_buf[(1, 0, 1, 2)[tile], at, :]

    def drag_terms(state, drag_here):
        square = state * state + 1.0
        root = lax.rsqrt(square)
        weak = drag_here * root
        return square, root, weak, weak * square

    for step in range(STEPS - 1):
        rows_beyond = RIM if STEPS + 5 - step > 8 else 8
        now, later = step % 2, (step + 1) % 2

        def advance(first, rows, step=step, now=now, later=later):
            at = pl.ds(first, rows)
            state = [u_buf[now, tile, at, :] for tile in range(LEV + 1)]
            sides = sideways(state[:LEV], state[LEV])
            mixed = upright(state[:LEV], state[LEV])
            for tile in range(LEV + 1):
                upwind = u_buf[now, tile, pl.ds(first - 1, rows), :]
                downwind = u_buf[now, tile, pl.ds(first + 1, rows), :]
                square, root, weak, strong = drag_terms(state[tile], drag_of(tile, at))
                centre = a_buf[tile, at, :] - strong
                u_buf[later, tile, at, :] = (
                    centre * state[tile]
                    + w_buf[tile, at, :] * upwind
                    + v_buf[tile, at, :] * (downwind + sides[tile])
                    + mixed[tile]
                )
                g_buf[step, tile, at, :] = centre - strong + weak
                if tile < LEV:
                    f_buf[step, tile, at, :] = state[tile] * (square * root)

        for_rows(TOP - rows_beyond, CX + 2 * rows_beyond, FORWARD_ROWS, advance)

    last = STEPS - 1

    def slopes(first, rows):
        at = pl.ds(first, rows)
        for tile in range(LEV + 1):
            state = u_buf[last % 2, tile, at, :]
            square, root, weak, strong = drag_terms(state, drag_of(tile, at))
            g_buf[last, tile, at, :] = a_buf[tile, at, :] - 2.0 * strong + weak
            if tile < LEV:
                f_buf[last, tile, at, :] = state * (square * root)

    for_rows(TOP - 8, CX + 16, FORWARD_ROWS, slopes)

    zero = jnp.zeros((CX + 16, CY), jnp.float32)
    for part in range(2):
        s_buf[part, TOP - 8 : TOP + CX + 8, :] = zero
    for step in reversed(range(STEPS)):
        rows_beyond = 8 if step else 0
        now, later = (last - step) % 2, (last - step + 1) % 2

        def retreat(first, rows, step=step, now=now, later=later):
            at = pl.ds(first, rows)
            before, after = pl.ds(first - 1, rows), pl.ds(first + 1, rows)
            adjoint = [l_buf[now, tile, at, :] for tile in range(LEV + 1)]
            flux = [v_buf[tile, at, :] * adjoint[tile] for tile in range(LEV + 1)]
            sides = sideways(flux[:LEV], flux[LEV])
            mixed = upright(adjoint[:LEV], adjoint[LEV] if step else None)
            for tile in range(LEV + 1 if step else LEV):
                value = (
                    g_buf[step, tile, at, :] * adjoint[tile]
                    + w_buf[tile, after, :] * l_buf[now, tile, after, :]
                    + v_buf[tile, before, :] * l_buf[now, tile, before, :]
                    + sides[tile]
                    + mixed[tile]
                )
                if step:
                    l_buf[later, tile, at, :] = value
                else:
                    start_ref[tile, pl.ds(first - TOP, rows), :] = value
            s_buf[0, at, :] += f_buf[step, 1, at, :] * adjoint[1]
            s_buf[1, at, :] += (
                f_buf[step, 0, at, :] * adjoint[0] + f_buf[step, 2, at, :] * adjoint[2]
            )

        for_rows(TOP - rows_beyond, CX + 2 * rows_beyond, ADJOINT_ROWS, retreat)

    inside = pl.ds(TOP, CX)
    sensitivity = s_buf[0, inside, :] + SIDE_GAIN * s_buf[1, inside, :]
    across = lax.dot_general(
        rows_buf[...], sensitivity, (((1,), (0,)), ((), ())),
        precision=lax.Precision.HIGHEST, preferred_element_type=jnp.float32,
    )
    sums = -jnp.sum(across * cols_buf[...], axis=1, keepdims=True)
    grads = jnp.zeros((devices, CY), jnp.float32)
    for k in range(per_device):
        mine = spread_lanes(sums[k * devices : (k + 1) * devices, :], devices)
        grads = jnp.where(lane == k, mine, grads)
    grads_ref[...] = grads


def shards(
    velocity, adjoint_seed, courant, viscosity, turbine_tile, turbine_offset, thrust, disk_width
):
    n_gx, n_gy = lax.axis_size("gx"), lax.axis_size("gy")
    devices = n_gx * n_gy
    per_device = thrust.shape[0]
    f32 = jnp.float32
    smem = pl.BlockSpec(memory_space=pltpu.SMEM)
    vmem = pl.BlockSpec(memory_space=pltpu.VMEM)

    def ring(axis, by):
        count = lax.axis_size(axis)
        return [(i, (i + by) % count) for i in range(count)]

    side_up, side_down, info = pl.pallas_call(
        functools.partial(pack_sides, n_gy),
        name="pack_sides",
        out_shape=(
            jax.ShapeDtypeStruct((SIDE_ROWS, CY), f32),
            jax.ShapeDtypeStruct((SIDE_ROWS, CY), f32),
            jax.ShapeDtypeStruct((devices, CY), f32),
        ),
        in_specs=[smem] * 4 + [vmem] * 4,
        out_specs=(vmem,) * 3,
    )(turbine_tile, turbine_offset, thrust, disk_width, velocity, adjoint_seed, courant, viscosity)
    west = lax.ppermute(side_up, "gy", ring("gy", 1))
    east = lax.ppermute(side_down, "gy", ring("gy", -1))
    info = lax.all_to_all(info, ("gx", "gy"), 0, 0, tiled=True)
    end_up, end_down = pl.pallas_call(
        pack_ends,
        name="pack_ends",
        out_shape=(jax.ShapeDtypeStruct((END_ROWS, CY), f32),) * 2,
        in_specs=[vmem] * 6,
        out_specs=(vmem,) * 2,
    )(west, east, velocity, adjoint_seed, courant, viscosity)
    low = lax.ppermute(end_up, "gx", ring("gx", 1))
    high = lax.ppermute(end_down, "gx", ring("gx", -1))
    place = jnp.stack([lax.axis_index("gx"), lax.axis_index("gy")]).astype(jnp.int32)
    turbines = devices * per_device
    adjoint_start, grads = pl.pallas_call(
        functools.partial(window, n_gx, n_gy, per_device),
        name="window",
        out_shape=(
            jax.ShapeDtypeStruct((LEV, CX, CY), f32),
            jax.ShapeDtypeStruct((devices, CY), f32),
        ),
        in_specs=[smem] + [vmem] * 9,
        out_specs=(vmem,) * 2,
        scratch_shapes=[
            pltpu.VMEM((2, LEV + 1, TALL, CY), f32),
            pltpu.VMEM((2, LEV + 1, TALL, CY), f32),
            pltpu.VMEM((STEPS, LEV + 1, TALL, CY), f32),
            pltpu.VMEM((STEPS, LEV, TALL, CY), f32),
            pltpu.VMEM((LEV + 1, TALL, CY), f32),
            pltpu.VMEM((LEV + 1, TALL, CY), f32),
            pltpu.VMEM((LEV + 1, TALL, CY), f32),
            pltpu.VMEM((3, TALL, CY), f32),
            pltpu.VMEM((2, TALL, CY), f32),
            pltpu.VMEM((turbines, CX), f32),
            pltpu.VMEM((turbines, CY), f32),
        ],
        compiler_params=pltpu.CompilerParams(vmem_limit_bytes=48 * 1024 * 1024),
    )(place, info, velocity, adjoint_seed, courant, viscosity, west, east, low, high)
    grads = lax.all_to_all(grads, ("gx", "gy"), 0, 0, tiled=True)
    return adjoint_start, jnp.sum(grads, axis=0)[:per_device]


def solution(mesh):
    tiled = P(None, "gx", "gy")
    spread = P(("gx", "gy"))
    matrix = P(("gx", "gy"), None)
    return jax.shard_map(
        shards,
        mesh=mesh,
        in_specs=(tiled, tiled, tiled, tiled, matrix, matrix, spread, spread),
        out_specs=(tiled, spread),
        check_vma=False,
    )
```

time: 697 us -> 69.3 us (0.10); the launches traced: 686 us -> 69.1 us
  local copies, waits for them, and re-layouts: 218 us -> 4.52 us
  blocking collectives: 181 us -> 11.7 us
  other arithmetic: 127 us -> 0.63 us
  starting transfers between devices: 64 us -> 12.9 us
  loops' own time: 46.2 us -> 0 us
  waiting for transfers between devices: 46.8 us -> 5.33 us
  Pallas kernels: 0 us -> 33.3 us
    unnamed x3 -> x0, blocking collectives: 115 us -> none
    sub x29 -> x0, other arithmetic: 76.8 us -> none  [the longest x6 32.3 us: advance(): center + advect * (upwind - center)]
    all_gather x1 -> x0, blocking collectives: 65.9 us -> none  [shards(): lax.all_gather(turbine_offset, ('gx', 'gy'), axis=0, tiled=True)]
    slice x59 -> x0, local copies, waits for them, and re-layouts: 60.4 us -> none  [the longest x37 34.9 us: padded_2(): lax.slice_in_dim(block, block.shape[dim] - width, None, axis=dim)]
    ppermute x64 -> x4, starting transfers between devices: 64 us -> 7.44 us  [the longest x1 3.54 us: shards(): high = lax.ppermute(end_down, 'gx', ring('gx', -1))]
    gather x41 -> x0, local copies, waits for them, and re-layouts: 53 us -> none
    another operation x2 -> x0, loops' own time: 46.2 us -> none  [the longest x1 46.2 us: shards(): lax.fori_loop(0, slot_count, add_turbine, jnp.zeros_like(velocity))]
    ppermute x32 -> x0, local copies, waits for them, and re-layouts: 45.4 us -> none  [the longest x16 24.7 us: padded_2(): lax.ppermute(lax.slice_in_dim(block, 0, width, axis=dim), axis, backward)]
  transfers between devices with their start and end apart: 64 -> 5, of which waited for: 36 -> 2; matrix products, arithmetic and copies ran while one was open for 31% -> 0% of each run, Pallas kernels for 0% -> 3%
where the time goes in v1:
time: 69.3 us; the launch traced here: 69.1 us
  Pallas kernels  33.3 us (48%)
  starting transfers between devices  12.9 us (19%)
  blocking collectives  11.7 us (17%)
  waiting for transfers between devices  5.33 us (8%)
  local copies, waits for them, and re-layouts  4.52 us (7%)
  between operations  0.74 us (1%)
    pallas_call x1, Pallas kernels, shards(): pl.pallas_call(functools.partial(window, n_gx, n_gy, per_device), name='w...  27.1 us
    all_to_all x1, blocking collectives, shards(): grads = lax.all_to_all(grads, ('gx', 'gy'), 0, 0, tiled=True)  11.7 us
    all_to_all x1, starting transfers between devices, shards(): info = lax.all_to_all(info, ('gx', 'gy'), 0, 0, tiled=True)  5.43 us
    unnamed x20, local copies, waits for them, and re-layouts  4.52 us
    pallas_call x1, Pallas kernels, shards(): pl.pallas_call(functools.partial(pack_sides, n_gy), name='pack_sides', ou...  4.02 us
    ppermute x1, starting transfers between devices, shards(): high = lax.ppermute(end_down, 'gx', ring('gx', -1))  3.54 us
    ppermute x1, starting transfers between devices, shards(): west = lax.ppermute(side_up, 'gy', ring('gy', 1))  2.94 us
    ppermute x1, waiting for transfers between devices, shards(): low = lax.ppermute(end_up, 'gx', ring('gx', 1))  2.66 us
  transfers between devices with their start and end apart: 5, of which 2 were waited for; matrix products, arithmetic and copies ran while one was open for 0% of the time, Pallas kernels for 3%

profile of v1, /device:TPU:0, one launch (start us, length us, event | category | flops | bytes accessed | tf_op | source)
XLA Modules:
  0.0 69.1 jit_solution(11989565528239108638)
XLA Ops:
  0.6 0.0 copy-start.8
  0.6 1.3 %copy.12.tile_ref = s32[4,1]{1,0:T(4,128)} copy(s32[4,1]{0,1:T(1,128)} %param.12) | data formatting | bytes 32 | tf_op args[4]
  2.0 0.0 copy-done.8
  2.0 0.7 copy.13.offset_ref
  2.6 4.0 %pack_sides.1 = (f32[320,128]{1,0:T(8,128)}, f32[320,128]{1,0:T(8,128)}, f32[32,128]{1,0:T(8,128)}) custom-call(s32[4,1]{1,0:T(4,128)} %copy.12.tile_ref, s32[4,2]{1,0:T(4,128)} %copy.13.offset_ref, f32[4]{0:T(128)} %thrust_ref.1, f32[4]{0:T(128)} %width_ref.1, f32[3,256,128]{2,1,0:T(8,128)} %vel_ref.5, f32[3,256,128]{2,1,0:T(8,128)} %seed_ref.5, ...), custom_call_target="tpu_custom_call" | custom-call | tf_op jit(solution)/shard_map/pack_sides/pallas_call | solution.py:393
  6.7 2.9 %collective-permute-start = (f32[320,128]{1,0:T(8,128)}, f32[320,128]{1,0:T(8,128)S(1)}, u32[]{:S(2)}, u32[]{:S(2)}) collective-permute-start(f32[320,128]{1,0:T(8,128)} %get-tuple-element.10), channel_id=1, source_target_pairs={{0,1},{1,2},{2,3},{3,0},{4,5},{5,6},{6,7},{7,4},{8,9},{9,10},{10,1... | collective-permute-start | bytes 491528 | tf_op jit(solution)/shard_map/ppermute | solution.py:404
  9.6 1.0 %collective-permute-start.1 = (f32[320,128]{1,0:T(8,128)}, f32[320,128]{1,0:T(8,128)S(1)}, u32[]{:S(2)}, u32[]{:S(2)}) collective-permute-start(f32[320,128]{1,0:T(8,128)} %get-tuple-element.11), channel_id=1, source_target_pairs={{0,3},{1,0},{2,1},{3,2},{4,7},{5,4},{6,5},{7,6},{8,11},{9,8},{10,9... | collective-permute-start | bytes 491528 | tf_op jit(solution)/shard_map/ppermute | solution.py:405
  10.6 5.4 %all-to-all-start = ((f32[32,1,128]{2,1,0:T(1,128)}), f32[32,1,128]{2,1,0:T(1,128)S(1)}, u32[]{:S(2)}, u32[]{:S(2)}) async-start(f32[32,1,128]{2,1,0:T(1,128)} %bitcast.12), calls=%async_computation | async-start | bytes 32768 | tf_op jit(solution)/shard_map/all_to_all | solution.py:406
  16.0 0.0 copy-start
  16.0 0.0 copy-start.1
  16.0 0.0 copy-start.2
  16.0 0.0 copy-start.3
  16.0 0.0 collective-permute-done.west_ref
  16.1 0.0 copy-start.4
  16.1 2.7 %collective-permute-done.1.east_ref = f32[320,128]{1,0:T(8,128)S(1)} collective-permute-done((f32[320,128]{1,0:T(8,128)}, f32[320,128]{1,0:T(8,128)S(1)}, u32[]{:S(2)}, u32[]{:S(2)}) %collective-permute-start.1) | collective-permute-done | bytes 163872 | tf_op jit(solution)/shard_map/ppermute | solution.py:405
  18.7 0.0 copy-done.4
  18.7 0.0 copy-start.6
  18.7 0.7 copy-done.6
  19.4 2.2 %pack_ends.1 = (f32[216,128]{1,0:T(8,128)}, f32[216,128]{1,0:T(8,128)}) custom-call(f32[320,128]{1,0:T(8,128)} %copy-done.4, f32[320,128]{1,0:T(8,128)} %copy-done.6, f32[3,256,128]{2,1,0:T(8,128)} %vel_ref.5, f32[3,256,128]{2,1,0:T(8,128)} %seed_ref.5, f32[3,256,128]{2,1,0:T(8,128)} %cou_ref.5, f32[3,256,128]{2,1,0:T(8,128)} %vis_ref.5), custom_call_target="tpu_custom_call" | custom-call | tf_op jit(solution)/shard_map/pack_ends/pallas_call | solution.py:407
  21.6 0.0 collective-permute-start.2
  21.6 3.5 %collective-permute-start.3 = (f32[216,128]{1,0:T(8,128)}, f32[216,128]{1,0:T(8,128)S(1)}, u32[]{:S(2)}, u32[]{:S(2)}) collective-permute-start(f32[216,128]{1,0:T(8,128)} %get-tuple-element.13), channel_id=1, source_target_pairs={{0,28},{4,0},{8,4},{12,8},{16,12},{20,16},{24,20},{28,24},{1,29},{... | collective-permute-start | bytes 331784 | tf_op jit(solution)/shard_map/ppermute | solution.py:415
  25.1 0.1 pad_add_fusion.place_ref
  25.2 0.0 all-to-all-done
  25.2 2.7 %collective-permute-done.2.low_ref = f32[216,128]{1,0:T(8,128)S(1)} collective-permute-done((f32[216,128]{1,0:T(8,128)}, f32[216,128]{1,0:T(8,128)S(1)}, u32[]{:S(2)}, u32[]{:S(2)}) %collective-permute-start.2) | collective-permute-done | bytes 110624 | tf_op jit(solution)/shard_map/ppermute | solution.py:414
  27.9 0.0 collective-permute-done.3.high_ref
  27.9 0.0 copy-done
  27.9 0.0 copy-done.1
  27.9 0.0 copy-done.2
  27.9 0.0 copy-done.3
  27.9 0.0 copy-start.5
  27.9 0.9 %copy-done.5 = f32[320,128]{1,0:T(8,128)S(1)} copy-done((f32[320,128]{1,0:T(8,128)S(1)}, f32[320,128]{1,0:T(8,128)}, u32[]{:S(2)}) %copy-start.5) | copy-done | bytes 163864
  28.8 0.0 copy-start.7
  28.8 0.9 %copy-done.7 = f32[320,128]{1,0:T(8,128)S(1)} copy-done((f32[320,128]{1,0:T(8,128)S(1)}, f32[320,128]{1,0:T(8,128)}, u32[]{:S(2)}) %copy-start.7) | copy-done | bytes 163864
  29.7 27.1 %window.1 = (f32[3,256,128]{2,1,0:T(8,128)}, f32[32,128]{1,0:T(8,128)S(1)}) custom-call(s32[2]{0:T(128)S(1)} %pad_add_fusion.place_ref, f32[32,128]{1,0:T(8,128)S(1)} %bitcast.10, f32[3,256,128]{2,1,0:T(8,128)S(1)} %copy-done, f32[3,256,128]{2,1,0:T(8,128)S(1)} %copy-done.1, f32[3,256,128]{2,1,0:T(8,128)S(1)} %copy-done.2, f32[3,256,128]{2,1,0:T(8,128)S(1)} %copy-done.3, ...), custom_call_target="tpu_custom_call" | custom-call | tf_op jit(solution)/shard_map/window/pallas_call | solution.py:418
  56.8 11.7 %all_to_all.20 = f32[32,1,128]{2,1,0:T(1,128)S(1)} all-to-all(f32[32,1,128]{2,1,0:T(1,128)S(1)} %bitcast.11), channel_id=1, replica_groups=mesh['gx'=8,'gy'=4] {'gx','gy'}, dimensions={0} | all-to-all | bytes 32768 | tf_op jit(solution)/shard_map/all_to_all | solution.py:442
  68.5 0.6 reduce_sum.9
Async XLA Ops:
  0.6 1.3 %copy-start.8 = (s32[4,2]{0,1:T(2,128)S(1)}, s32[4,2]{0,1:T(2,128)}, u32[]{:S(2)}) copy-start(s32[4,2]{0,1:T(2,128)} %param.13) | copy-start | bytes 100
  6.7 9.4 %collective-permute-start = (f32[320,128]{1,0:T(8,128)}, f32[320,128]{1,0:T(8,128)S(1)}, u32[]{:S(2)}, u32[]{:S(2)}) collective-permute-start(f32[320,128]{1,0:T(8,128)} %get-tuple-element.10), channel_id=1, source_target_pairs={{0,1},{1,2},{2,3},{3,0},{4,5},{5,6},{6,7},{7,4},{8,9},{9,10},{10,1... | collective-permute-start | bytes 491528 | tf_op jit(solution)/shard_map/ppermute | solution.py:404
  9.6 9.1 %collective-permute-start.1 = (f32[320,128]{1,0:T(8,128)}, f32[320,128]{1,0:T(8,128)S(1)}, u32[]{:S(2)}, u32[]{:S(2)}) collective-permute-start(f32[320,128]{1,0:T(8,128)} %get-tuple-element.11), channel_id=1, source_target_pairs={{0,3},{1,0},{2,1},{3,2},{4,7},{5,4},{6,5},{7,6},{8,11},{9,8},{10,9... | collective-permute-start | bytes 491528 | tf_op jit(solution)/shard_map/ppermute | solution.py:405
  10.6 14.6 %all-to-all-start = ((f32[32,1,128]{2,1,0:T(1,128)}), f32[32,1,128]{2,1,0:T(1,128)S(1)}, u32[]{:S(2)}, u32[]{:S(2)}) async-start(f32[32,1,128]{2,1,0:T(1,128)} %bitcast.12), calls=%async_computation | async-start | bytes 32768 | tf_op jit(solution)/shard_map/all_to_all | solution.py:406
  16.0 11.9 %copy-start = (f32[3,256,128]{2,1,0:T(8,128)S(1)}, f32[3,256,128]{2,1,0:T(8,128)}, u32[]{:S(2)}) copy-start(f32[3,256,128]{2,1,0:T(8,128)} %vel_ref.5) | copy-start | bytes 1179652
  16.0 11.9 %copy-start.1 = (f32[3,256,128]{2,1,0:T(8,128)S(1)}, f32[3,256,128]{2,1,0:T(8,128)}, u32[]{:S(2)}) copy-start(f32[3,256,128]{2,1,0:T(8,128)} %seed_ref.5) | copy-start | bytes 1179652
  16.0 11.9 %copy-start.2 = (f32[3,256,128]{2,1,0:T(8,128)S(1)}, f32[3,256,128]{2,1,0:T(8,128)}, u32[]{:S(2)}) copy-start(f32[3,256,128]{2,1,0:T(8,128)} %cou_ref.5) | copy-start | bytes 1179652
  16.0 11.9 %copy-start.3 = (f32[3,256,128]{2,1,0:T(8,128)S(1)}, f32[3,256,128]{2,1,0:T(8,128)}, u32[]{:S(2)}) copy-start(f32[3,256,128]{2,1,0:T(8,128)} %vis_ref.5) | copy-start | bytes 1179652
  16.1 2.7 %copy-start.4 = (f32[320,128]{1,0:T(8,128)}, f32[320,128]{1,0:T(8,128)S(1)}, u32[]{:S(2)}) copy-start(f32[320,128]{1,0:T(8,128)S(1)} %collective-permute-done.west_ref) | copy-start | bytes 491524
  18.7 0.7 copy-start.6
  21.6 6.3 %collective-permute-start.2 = (f32[216,128]{1,0:T(8,128)}, f32[216,128]{1,0:T(8,128)S(1)}, u32[]{:S(2)}, u32[]{:S(2)}) collective-permute-start(f32[216,128]{1,0:T(8,128)} %get-tuple-element.12), channel_id=1, source_target_pairs={{0,4},{4,8},{8,12},{12,16},{16,20},{20,24},{24,28},{28,0},{1,5},{5... | collective-permute-start | bytes 331784 | tf_op jit(solution)/shard_map/ppermute | solution.py:414
  21.6 6.3 %collective-permute-start.3 = (f32[216,128]{1,0:T(8,128)}, f32[216,128]{1,0:T(8,128)S(1)}, u32[]{:S(2)}, u32[]{:S(2)}) collective-permute-start(f32[216,128]{1,0:T(8,128)} %get-tuple-element.13), channel_id=1, source_target_pairs={{0,28},{4,0},{8,4},{12,8},{16,12},{20,16},{24,20},{28,24},{1,29},{... | collective-permute-start | bytes 331784 | tf_op jit(solution)/shard_map/ppermute | solution.py:415
  27.9 0.9 %copy-start.5 = (f32[320,128]{1,0:T(8,128)S(1)}, f32[320,128]{1,0:T(8,128)}, u32[]{:S(2)}) copy-start(f32[320,128]{1,0:T(8,128)} %copy-done.4) | copy-start | bytes 491524
  28.8 0.9 %copy-start.7 = (f32[320,128]{1,0:T(8,128)S(1)}, f32[320,128]{1,0:T(8,128)}, u32[]{:S(2)}) copy-start(f32[320,128]{1,0:T(8,128)} %copy-done.6) | copy-start | bytes 491524

commit v2 on v1

v2 whole, which is shorter than its diff:
```python
import functools
import math

import jax
import jax.numpy as jnp
from jax import lax
from jax.experimental import pallas as pl
from jax.experimental.pallas import tpu as pltpu
from jax.sharding import PartitionSpec as P

STEPS = 8
FP = 64
VERTICAL_MIX = 0.05
DRAG_SCALE = 0.01
SIDE_GAIN = math.exp(-0.5)

LEV, CX, CY = 3, 256, 128
WIDE = 14
MID = 13
THIN = 8
GAP = 42
RIM = 16
TOP = 24
TALL = CX + 2 * TOP
SIDE_ROWS = CX + 64
END_ROWS = 3 * LEV * RIM + LEV * THIN + 2 * RIM + 2 * THIN
VALUES = 6
CHUNK = 32
AHEAD = 2
SMALL = pltpu.CompilerParams(vmem_limit_bytes=8 * 1024 * 1024)


def lane_ids():
    return lax.broadcasted_iota(jnp.int32, (1, CY), 1)


def spread_lanes(value, rows):
    return jnp.broadcast_to(value, (rows, CY))


def rolled(value, shift):
    shift = shift % CY
    return value if shift == 0 else pltpu.roll(value, shift, 1)


def rim_place(lane):
    level = jnp.where((lane >= GAP // 2) & (lane < GAP // 2 + GAP), 1, 0)
    level = jnp.where((lane >= GAP // 2 + GAP) & (lane < GAP // 2 + 2 * GAP), 2, level)
    place = lane - GAP * level
    place = jnp.where(lane >= GAP // 2 + 2 * GAP, lane - CY, place)
    return level, place


def for_rows(first, count, chunk, body):
    full = count // chunk
    if full == 1:
        body(first, chunk)
    elif full > 1:

        def one(index, carry):
            body(pl.multiple_of(first + index * chunk, 8), chunk)
            return carry

        lax.fori_loop(0, full, one, 0)
    if count > full * chunk:
        body(first + full * chunk, count - full * chunk)


def pack_sides(
    n_gy, tile_hbm, offset_hbm, thrust_hbm, width_hbm, vel_hbm, seed_hbm, cou_hbm, vis_hbm,
    up_ref, down_ref, info_ref,
    tile_ref, offset_ref, thrust_ref, width_ref, vel_ref, seed_ref, cou_ref, vis_ref, arrived,
):
    copies = [
        pltpu.make_async_copy(source, target, arrived.at[index])
        for index, (source, target) in enumerate(
            (
                (seed_hbm, seed_ref), (vel_hbm, vel_ref), (cou_hbm, cou_ref), (vis_hbm, vis_ref),
                (tile_hbm, tile_ref), (offset_hbm, offset_ref), (thrust_hbm, thrust_ref),
                (width_hbm, width_ref),
            )
        )
    ]
    for copy in copies:
        copy.start()
    lane = lane_ids()
    level_of, _ = rim_place(lane)
    for copy in copies[4:]:
        copy.wait()
    whole = jnp.zeros((1, CY), jnp.int32)
    real = jnp.zeros((1, CY), jnp.float32)
    for k in range(thrust_ref.shape[0]):
        tile = tile_ref[k]
        for spot, value in enumerate(
            (tile // n_gy, tile % n_gy, offset_ref[0, k], offset_ref[1, k])
        ):
            whole = jnp.where(lane == VALUES * k + spot, value, whole)
        real = jnp.where(lane == VALUES * k + 4, thrust_ref[k], real)
        real = jnp.where(lane == VALUES * k + 5, width_ref[k], real)
    info_ref[...] = jnp.broadcast_to(whole.astype(jnp.float32) + real, info_ref.shape)

    copies[0].wait()
    for out_ref, low in ((up_ref, False), (down_ref, True)):
        total = jnp.zeros((64, CY), jnp.float32)
        for block in range(4):
            for level in range(LEV):
                to = 32 * block + THIN * level
                moved = rolled(
                    seed_ref[level, 64 * block : 64 * block + 64, :],
                    to - (0 if low else CY - THIN),
                )
                total = jnp.where((lane >= to) & (lane < to + THIN), moved, total)
        out_ref[CX:SIDE_ROWS, :] = total

    def around(ref):
        value = jnp.where(level_of == 1, rolled(ref[1], GAP), ref[0])
        return jnp.where(level_of == 2, rolled(ref[2], 2 * GAP), value)

    up = down = None
    for index, (ref, width) in enumerate(((vel_ref, WIDE), (cou_ref, MID), (vis_ref, MID))):
        copies[1 + index].wait()
        both = around(ref)
        start = (0, WIDE, WIDE + MID)[index]
        if index == 0:
            up, down = rolled(both, width), both
        else:
            mine = in_share(lane, start, width)
            up = jnp.where(mine, rolled(both, start + width), up)
            down = jnp.where(mine, rolled(both, start), down)
    up_ref[0:CX, :] = up
    down_ref[0:CX, :] = down


def in_share(lane, start, width):
    inside = jnp.zeros(lane.shape, jnp.bool_)
    for level in range(LEV):
        first = GAP * level + start
        inside = inside | ((lane >= first) & (lane < first + width))
    return inside


def pack_ends(west_ref, east_ref, vel_ref, seed_ref, cou_ref, vis_ref, up_ref, down_ref):
    for out_ref, low in ((up_ref, False), (down_ref, True)):
        at = 0
        first = 0 if low else CX - RIM
        for ref in (vel_ref, cou_ref, vis_ref):
            for level in range(LEV):
                out_ref[at : at + RIM, :] = ref[level, first : first + RIM, :]
                at += RIM
        thin_first = 0 if low else CX - THIN
        for level in range(LEV):
            out_ref[at : at + THIN, :] = seed_ref[level, thin_first : thin_first + THIN, :]
            at += THIN
        for ref in (west_ref, east_ref):
            out_ref[at : at + RIM, :] = ref[first : first + RIM, :]
            at += RIM
        side_first = CX if low else SIDE_ROWS - THIN
        for ref in (west_ref, east_ref):
            out_ref[at : at + THIN, :] = ref[side_first : side_first + THIN, :]
            at += THIN


def level_mix(level):
    return VERTICAL_MIX * (2 if level == 1 else 1)


def rim_mixes():
    level_of, place = rim_place(lane_ids())
    valid = (place >= -WIDE) & (place < WIDE)
    from_above = jnp.where(valid & (level_of < LEV - 1), VERTICAL_MIX, 0.0).astype(jnp.float32)
    from_below = jnp.where(valid & (level_of > 0), VERTICAL_MIX, 0.0).astype(jnp.float32)
    return valid, from_above, from_below


def put_coefficients(bufs, tile, to, rows, courant, viscosity, mix):
    a_buf, w_buf, v_buf = bufs
    a_buf[tile, pl.ds(to, rows), :] = 1.0 - courant - 4.0 * viscosity - mix
    w_buf[tile, pl.ds(to, rows), :] = courant + viscosity
    v_buf[tile, pl.ds(to, rows), :] = viscosity


def put_rim(u_buf, bufs, west, east, to, rows):
    _, place = rim_place(lane_ids())
    _, from_above, from_below = rim_mixes()
    zero = jnp.zeros((rows, CY), jnp.float32)
    start = 0
    found = []
    for width in (WIDE, MID, MID):
        value = jnp.where((place >= 0) & (place < width), rolled(east, -start), zero)
        found.append(
            jnp.where((place >= -width) & (place < 0), rolled(west, -start - width), value)
        )
        start += width
    u_buf[LEV, pl.ds(to, rows), :] = found[0]
    put_coefficients(bufs, LEV, to, rows, found[1], found[2], from_above + from_below)


def put_thin_rim(l_buf, west, east, block, to, rows):
    level_of, place = rim_place(lane_ids())
    value = jnp.zeros((rows, CY), jnp.float32)
    for level in range(LEV):
        at = GAP * level - (32 * block + THIN * level)
        mine = level_of == level
        value = jnp.where(mine & (place >= 0) & (place < THIN), rolled(east, at), value)
        value = jnp.where(mine & (place >= -THIN) & (place < 0), rolled(west, at - THIN), value)
    l_buf[LEV, pl.ds(to, rows), :] = value


def prepare(
    n_gx, n_gy, per_device,
    place_ref, info_ref, vel_ref, seed_ref, cou_ref, vis_ref, west_ref, east_ref,
    u_buf, l_buf, a_buf, w_buf, v_buf, d_buf, rows_buf, cols_buf,
):
    lane = lane_ids()
    level_of, place = rim_place(lane)
    level_one = level_of == 1
    valid, _, _ = rim_mixes()

    devices = info_ref.shape[0]
    my_gx = place_ref[0].astype(jnp.float32)
    my_gy = place_ref[1].astype(jnp.float32)
    col_of = jnp.where(place < 0, place, CY + place).astype(jnp.float32)
    row_lane = lax.broadcasted_iota(jnp.int32, (1, 3 * CY), 1).astype(jnp.float32)
    row_profiles, rim_profiles = [], []

    def near(delta, count):
        delta = jnp.where(delta >= count / 2, delta - count, delta)
        return jnp.where(delta < -count / 2, delta + count, delta)

    def profile(cells, first, width):
        at = cells - first
        centred = at - (FP - 1) / 2.0
        value = jnp.exp(-(centred * centred) / (2.0 * width * width))
        return jnp.where((at >= 0.0) & (at < float(FP)), value, 0.0)

    for k in range(per_device):
        info = info_ref[:, VALUES * k : VALUES * k + VALUES]
        row_first = near(info[:, 0:1] - my_gx, n_gx) * CX + info[:, 2:3]
        col_first = near(info[:, 1:2] - my_gy, n_gy) * CY + info[:, 3:4]
        scale = DRAG_SCALE * info[:, 4:5]
        width = info[:, 5:6]
        part = pl.ds(k * devices, devices)
        row_profiles.append(profile(row_lane - RIM, row_first, width) * scale)
        rows_buf[part, :] = profile(row_lane[:, :CX], row_first, width) * scale
        cols_buf[part, :] = profile(lane.astype(jnp.float32), col_first, width)
        rim_profiles.append(profile(col_of, col_first, width))
    along_rows = jnp.concatenate(row_profiles, axis=0)
    along_cols = jnp.concatenate([cols_buf[...], jnp.concatenate(rim_profiles, axis=0)], axis=1)
    drag = lax.dot_general(
        along_rows.T, along_cols, (((1,), (0,)), ((), ())),
        precision=lax.Precision.HIGHEST, preferred_element_type=jnp.float32,
    )
    tall = pl.ds(TOP - RIM, CX + 2 * RIM)
    gain = jnp.where(valid, jnp.where(level_one, 1.0, SIDE_GAIN), 0.0).astype(jnp.float32)
    d_buf[0, tall, :] = drag[: CX + 2 * RIM, :CY]
    d_buf[1, tall, :] = drag[: CX + 2 * RIM, :CY] * SIDE_GAIN
    d_buf[2, tall, :] = drag[: CX + 2 * RIM, CY:] * gain

    edge = jnp.zeros((TOP - RIM, CY), jnp.float32)
    for tile in range(LEV + 1):
        for buf in (a_buf, w_buf, v_buf, u_buf, l_buf):
            buf[tile, 0 : TOP - RIM, :] = edge
            buf[tile, TALL - TOP + RIM :, :] = edge
        l_buf[tile, TOP - RIM : TOP - THIN, :] = edge
        l_buf[tile, TOP + CX + THIN : TOP + CX + RIM, :] = edge
    inside = pl.ds(TOP, CX)
    bufs = (a_buf, w_buf, v_buf)
    for level in range(LEV):
        u_buf[level, inside, :] = vel_ref[level]
        l_buf[level, inside, :] = seed_ref[level]
        put_coefficients(bufs, level, TOP, CX, cou_ref[level], vis_ref[level], level_mix(level))
    put_rim(u_buf, bufs, west_ref[0:CX, :], east_ref[0:CX, :], TOP, CX)
    for block in range(4):
        at = pl.ds(CX, 64)
        put_thin_rim(l_buf, west_ref[at, :], east_ref[at, :], block, TOP + 64 * block, 64)


def window(
    per_device,
    u_even_in, l_even_in, a_in, w_in, v_in, d_buf, rows_buf, cols_buf, low_ref, high_ref,
    start_ref, grads_ref, u_even, l_even, a_buf, w_buf, v_buf,
    u_odd, l_odd, g_buf, f_buf, s_buf,
):
    u_buf, l_buf = (u_even, u_odd), (l_even, l_odd)
    bufs = (a_buf, w_buf, v_buf)
    lane = lane_ids()
    level_of, place = rim_place(lane)
    west_lane, east_lane = place == -1, place == 0
    level_one, level_two = level_of == 1, level_of == 2
    _, from_above, from_below = rim_mixes()
    first_lane, last_lane = lane == 0, lane == CY - 1
    devices = grads_ref.shape[0]

    edge = jnp.zeros((TOP - RIM, CY), jnp.float32)
    for tile in range(LEV + 1):
        for buf in (u_odd, l_odd):
            buf[tile, 0 : TOP - RIM, :] = edge
            buf[tile, TALL - TOP + RIM :, :] = edge
        l_odd[tile, TOP - RIM : TOP - THIN, :] = edge
        l_odd[tile, TOP + CX + THIN : TOP + CX + RIM, :] = edge
    for ref, to, thin_to, block in (
        (low_ref, TOP - RIM, TOP - THIN, 3),
        (high_ref, TOP + CX, TOP + CX, 0),
    ):
        for level in range(LEV):
            u_even[level, to : to + RIM, :] = ref[RIM * level : RIM * level + RIM, :]
            courant = ref[RIM * (LEV + level) : RIM * (LEV + level) + RIM, :]
            viscosity = ref[RIM * (2 * LEV + level) : RIM * (2 * LEV + level) + RIM, :]
            put_coefficients(bufs, level, to, RIM, courant, viscosity, level_mix(level))
            at = 3 * LEV * RIM + THIN * level
            l_even[level, thin_to : thin_to + THIN, :] = ref[at : at + THIN, :]
        at = 3 * LEV * RIM + LEV * THIN
        put_rim(u_even, bufs, ref[at : at + RIM, :], ref[at + RIM : at + 2 * RIM, :], to, RIM)
        at += 2 * RIM
        west, east = ref[at : at + THIN, :], ref[at + THIN : at + 2 * THIN, :]
        put_thin_rim(l_even, west, east, block, thin_to, THIN)

    def borders(tiles):
        packed = tiles[LEV]
        across = [rolled(packed, -GAP * level) for level in range(LEV)]
        other = jnp.where(level_one, rolled(tiles[1], GAP), tiles[0])
        across.append(jnp.where(level_two, rolled(tiles[2], 2 * GAP), other))
        return across

    def sideways(tiles, across, with_rim=True):
        sums = []
        for tile in range(LEV + 1 if with_rim else LEV):
            low, high = (west_lane, east_lane) if tile == LEV else (last_lane, first_lane)
            left = rolled(jnp.where(low, across[tile], tiles[tile]), 1)
            right = rolled(jnp.where(high, across[tile], tiles[tile]), -1)
            sums.append(left + right)
        return sums

    def upright(core):
        middle = VERTICAL_MIX * core[1]
        return [middle, VERTICAL_MIX * (core[0] + core[2]), middle]

    def rim_upright(packed):
        return from_above * rolled(packed, -GAP) + from_below * rolled(packed, GAP)

    def drag_of(tile, at):
        return d_buf[(1, 0, 1, 2)[tile], at, :]

    def drag_terms(state, drag_here):
        square = state * state + 1.0
        root = lax.rsqrt(square)
        weak = drag_here * root
        return square, root, weak, weak * square

    def staged(first, count, stages):
        chunks = [(first + at, min(CHUNK, count - at)) for at in range(0, count, CHUNK)]
        held = [None] * len(chunks)
        delay = (len(stages) - 1) * AHEAD
        for tick in range(len(chunks) + delay):
            for index, stage in enumerate(stages):
                at = tick - index * AHEAD
                if 0 <= at < len(chunks):
                    held[at] = stage(pl.ds(*chunks[at]), chunks[at], held[at])

    for step in range(STEPS - 1):
        rows_beyond = RIM if STEPS + 5 - step > 8 else 8
        now, later = step % 2, (step + 1) % 2

        def exchange(at, chunk, _, now=now):
            return borders([u_buf[now][tile, at, :] for tile in range(LEV + 1)])

        def shift(at, chunk, other, now=now):
            state = [u_buf[now][tile, at, :] for tile in range(LEV + 1)]
            return sideways(state, other), rim_upright(state[LEV])

        def advance(at, chunk, shifted, step=step, now=now, later=later):
            first, rows = chunk
            sides, mixed_rim = shifted
            state = [u_buf[now][tile, at, :] for tile in range(LEV + 1)]
            mixed = upright(state) + [mixed_rim]
            for tile in range(LEV + 1):
                upwind = u_buf[now][tile, pl.ds(first - 1, rows), :]
                downwind = u_buf[now][tile, pl.ds(first + 1, rows), :]
                square, root, weak, strong = drag_terms(state[tile], drag_of(tile, at))
                centre = a_buf[tile, at, :] - strong
                u_buf[later][tile, at, :] = (
                    centre * state[tile]
                    + w_buf[tile, at, :] * upwind
                    + v_buf[tile, at, :] * (downwind + sides[tile])
                    + mixed[tile]
                )
                g_buf[step, tile, at, :] = centre - strong + weak
                if tile < LEV:
                    f_buf[step, tile, at, :] = state[tile] * (square * root)

        staged(TOP - rows_beyond, CX + 2 * rows_beyond, (exchange, shift, advance))

    last = STEPS - 1

    def slopes(first, rows):
        at = pl.ds(first, rows)
        for tile in range(LEV + 1):
            state = u_buf[last % 2][tile, at, :]
            square, root, weak, strong = drag_terms(state, drag_of(tile, at))
            g_buf[last, tile, at, :] = a_buf[tile, at, :] - 2.0 * strong + weak
            if tile < LEV:
                f_buf[last, tile, at, :] = state * (square * root)

    for_rows(TOP - 8, CX + 16, CX + 16, slopes)

    zero = jnp.zeros((CX + 16, CY), jnp.float32)
    for part in range(2):
        s_buf[part, TOP - 8 : TOP + CX + 8, :] = zero
    for step in reversed(range(STEPS)):
        rows_beyond = 8 if step else 0
        now, later = (last - step) % 2, (last - step + 1) % 2

        def fluxes(at, now=now):
            adjoint = [l_buf[now][tile, at, :] for tile in range(LEV + 1)]
            return adjoint, [v_buf[tile, at, :] * adjoint[tile] for tile in range(LEV + 1)]

        def exchange(at, chunk, _, fluxes=fluxes):
            return borders(fluxes(at)[1])

        def shift(at, chunk, other, fluxes=fluxes, step=step):
            adjoint, flux = fluxes(at)
            return sideways(flux, other, bool(step)), rim_upright(adjoint[LEV]) if step else None

        def retreat(at, chunk, shifted, step=step, now=now, later=later):
            first, rows = chunk
            sides, mixed_rim = shifted
            before, after = pl.ds(first - 1, rows), pl.ds(first + 1, rows)
            adjoint = [l_buf[now][tile, at, :] for tile in range(LEV + 1)]
            mixed = upright(adjoint) + [mixed_rim]
            for tile in range(LEV + 1 if step else LEV):
                value = (
                    g_buf[step, tile, at, :] * adjoint[tile]
                    + w_buf[tile, after, :] * l_buf[now][tile, after, :]
                    + v_buf[tile, before, :] * l_buf[now][tile, before, :]
                    + sides[tile]
                    + mixed[tile]
                )
                if step:
                    l_buf[later][tile, at, :] = value
                else:
                    start_ref[tile, pl.ds(first - TOP, rows), :] = value
            s_buf[0, at, :] += f_buf[step, 1, at, :] * adjoint[1]
            s_buf[1, at, :] += (
                f_buf[step, 0, at, :] * adjoint[0] + f_buf[step, 2, at, :] * adjoint[2]
            )

        staged(TOP - rows_beyond, CX + 2 * rows_beyond, (exchange, shift, retreat))

    inside = pl.ds(TOP, CX)
    sensitivity = s_buf[0, inside, :] + SIDE_GAIN * s_buf[1, inside, :]
    across = lax.dot_general(
        rows_buf[...], sensitivity, (((1,), (0,)), ((), ())),
        precision=lax.Precision.HIGHEST, preferred_element_type=jnp.float32,
    )
    sums = -jnp.sum(across * cols_buf[...], axis=1, keepdims=True)
    grads = jnp.zeros((devices, CY), jnp.float32)
    for k in range(per_device):
        mine = spread_lanes(sums[k * devices : (k + 1) * devices, :], devices)
        grads = jnp.where(lane == k, mine, grads)
    grads_ref[...] = grads


def shards(
    velocity, adjoint_seed, courant, viscosity, turbine_tile, turbine_offset, thrust, disk_width
):
    n_gx, n_gy = lax.axis_size("gx"), lax.axis_size("gy")
    devices = n_gx * n_gy
    per_device = thrust.shape[0]
    f32 = jnp.float32
    smem = pl.BlockSpec(memory_space=pltpu.SMEM)
    vmem = pl.BlockSpec(memory_space=pltpu.VMEM)

    def ring(axis, by):
        count = lax.axis_size(axis)
        return [(i, (i + by) % count) for i in range(count)]

    side_up, side_down, info = pl.pallas_call(
        functools.partial(pack_sides, n_gy),
        name="pack_sides",
        out_shape=(
            jax.ShapeDtypeStruct((SIDE_ROWS, CY), f32),
            jax.ShapeDtypeStruct((SIDE_ROWS, CY), f32),
            jax.ShapeDtypeStruct((devices, CY), f32),
        ),
        in_specs=[pl.BlockSpec(memory_space=pl.ANY)] * 8,
        out_specs=(vmem,) * 3,
        scratch_shapes=[
            pltpu.SMEM((per_device,), jnp.int32),
            pltpu.SMEM((2, per_device), jnp.int32),
            pltpu.SMEM((per_device,), f32),
            pltpu.SMEM((per_device,), f32),
            *[pltpu.VMEM((LEV, CX, CY), f32)] * 4,
            pltpu.SemaphoreType.DMA((8,)),
        ],
    )(turbine_tile.reshape(per_device), turbine_offset.T, thrust, disk_width, velocity, adjoint_seed, courant, viscosity)
    west = lax.ppermute(side_up, "gy", ring("gy", 1))
    east = lax.ppermute(side_down, "gy", ring("gy", -1))
    info = lax.all_to_all(info, ("gx", "gy"), 0, 0, tiled=True)
    end_up, end_down = pl.pallas_call(
        pack_ends,
        name="pack_ends",
        out_shape=(jax.ShapeDtypeStruct((END_ROWS, CY), f32),) * 2,
        in_specs=[vmem] * 6,
        out_specs=(vmem,) * 2,
        compiler_params=SMALL,
    )(west, east, velocity, adjoint_seed, courant, viscosity)
    low = lax.ppermute(end_up, "gx", ring("gx", 1))
    high = lax.ppermute(end_down, "gx", ring("gx", -1))
    place = jnp.stack([lax.axis_index("gx"), lax.axis_index("gy")]).astype(jnp.int32)
    turbines = devices * per_device
    field = jax.ShapeDtypeStruct((LEV + 1, TALL, CY), f32)
    fields = pl.pallas_call(
        functools.partial(prepare, n_gx, n_gy, per_device),
        name="prepare",
        out_shape=(
            *[field] * 5,
            jax.ShapeDtypeStruct((3, TALL, CY), f32),
            jax.ShapeDtypeStruct((turbines, CX), f32),
            jax.ShapeDtypeStruct((turbines, CY), f32),
        ),
        in_specs=[smem] + [vmem] * 7,
        out_specs=(vmem,) * 8,
        compiler_params=SMALL,
        cost_estimate=pl.CostEstimate(flops=40000000, bytes_accessed=8000000, transcendentals=0),
    )(place, info, velocity, adjoint_seed, courant, viscosity, west, east)
    adjoint_start, grads, *_ = pl.pallas_call(
        functools.partial(window, per_device),
        name="window",
        out_shape=(
            jax.ShapeDtypeStruct((LEV, CX, CY), f32),
            jax.ShapeDtypeStruct((devices, CY), f32),
            *[field] * 5,
        ),
        in_specs=[vmem] * 10,
        out_specs=(vmem,) * 7,
        input_output_aliases={index: index + 2 for index in range(5)},
        scratch_shapes=[
            pltpu.VMEM((LEV + 1, TALL, CY), f32),
            pltpu.VMEM((LEV + 1, TALL, CY), f32),
            pltpu.VMEM((STEPS, LEV + 1, TALL, CY), f32),
            pltpu.VMEM((STEPS, LEV, TALL, CY), f32),
            pltpu.VMEM((2, TALL, CY), f32),
        ],
        compiler_params=pltpu.CompilerParams(vmem_limit_bytes=24 * 1024 * 1024),
    )(*fields, low, high)
    grads = lax.all_to_all(grads, ("gx", "gy"), 0, 0, tiled=True)
    return adjoint_start, jnp.sum(grads, axis=0)[:per_device]


def solution(mesh):
    tiled = P(None, "gx", "gy")
    spread = P(("gx", "gy"))
    matrix = P(("gx", "gy"), None)
    return jax.shard_map(
        shards,
        mesh=mesh,
        in_specs=(tiled, tiled, tiled, tiled, matrix, matrix, spread, spread),
        out_specs=(tiled, spread),
        check_vma=False,
    )
```

time: 69.3 us -> 43.1 us (0.62)
  Pallas kernels: 33.3 us -> 13.2 us
  local copies, waits for them, and re-layouts: 4.52 us -> 0.02 us
  waiting for transfers between devices: 5.33 us -> 3.69 us
    pallas_call x1 -> x2, Pallas kernels: 27.1 us -> 10.3 us  [the longest x1 8.86 us: shards(): pl.pallas_call(functools.partial(window, per_device), name='window', out_...]
    unnamed x20 -> x8, local copies, waits for them, and re-layouts: 4.52 us -> 0.02 us
    ppermute x1, waiting for transfers between devices: 2.66 us -> 0.25 us  [shards(): low = lax.ppermute(end_up, 'gx', ring('gx', 1))]
    pallas_call x1, Pallas kernels: 2.18 us -> 0.02 us  [shards(): pl.pallas_call(pack_ends, name='pack_ends', out_shape=(jax.ShapeDtypeStru...]
    pallas_call x1, Pallas kernels: 4.02 us -> 2.84 us  [shards(): pl.pallas_call(functools.partial(pack_sides, n_gy), name='pack_sides', ou...]
    all_to_all x1, waiting for transfers between devices: 0.01 us -> 0.72 us  [shards(): info = lax.all_to_all(info, ('gx', 'gy'), 0, 0, tiled=True)]
  transfers between devices with their start and end apart: 5 -> 5, of which waited for: 2 -> 3; matrix products, arithmetic and copies ran while one was open for 0% -> 0% of each run, Pallas kernels for 3% -> 3%
where the time goes in v2:
time: 43.1 us; the launch traced here: 42.9 us
  Pallas kernels  13.2 us (31%)
  starting transfers between devices  13 us (30%)
  blocking collectives  11.7 us (27%)
  waiting for transfers between devices  3.69 us (9%)
  between operations  0.73 us (2%)
  other arithmetic  0.63 us (1%)
    all_to_all x1, blocking collectives, shards(): grads = lax.all_to_all(grads, ('gx', 'gy'), 0, 0, tiled=True)  11.7 us
    pallas_call x1, Pallas kernels, shards(): pl.pallas_call(functools.partial(window, per_device), name='window', out_...  8.86 us
    all_to_all x1, starting transfers between devices, shards(): info = lax.all_to_all(info, ('gx', 'gy'), 0, 0, tiled=True)  5.36 us
    ppermute x1, starting transfers between devices, shards(): high = lax.ppermute(end_down, 'gx', ring('gx', -1))  3.53 us
    ppermute x1, starting transfers between devices, shards(): west = lax.ppermute(side_up, 'gy', ring('gy', 1))  2.99 us
    pallas_call x1, Pallas kernels, shards(): pl.pallas_call(functools.partial(pack_sides, n_gy), name='pack_sides', ou...  2.84 us
    ppermute x1, waiting for transfers between devices, shards(): east = lax.ppermute(side_down, 'gy', ring('gy', -1))  2.72 us
    pallas_call x1, Pallas kernels, shards(): pl.pallas_call(functools.partial(prepare, n_gx, n_gy, per_device), name='...  1.48 us
  transfers between devices with their start and end apart: 5, of which 3 were waited for; matrix products, arithmetic and copies ran while one was open for 0% of the time, Pallas kernels for 3%

profile of v2, /device:TPU:0, one launch (start us, length us, event | category | flops | bytes accessed | tf_op | source)
XLA Modules:
  0.0 42.9 jit_solution(14925186219431806692)
XLA Ops:
  0.6 0.0 copy-start
  0.6 0.0 copy-start.1
  0.7 0.0 copy-start.2
  0.7 0.0 copy-start.3
  0.7 2.8 %pack_sides.1 = (f32[320,128]{1,0:T(8,128)}, f32[320,128]{1,0:T(8,128)}, f32[32,128]{1,0:T(8,128)}) custom-call(s32[4]{0:T(128)} %bitcast.16, s32[2,4]{1,0:T(2,128)} %bitcast.15, f32[4]{0:T(128)} %thrust_hbm.1, f32[4]{0:T(128)} %width_hbm.1, f32[3,256,128]{2,1,0:T(8,128)} %vel_ref.3, f32[3,256,128]{2,1,0:T(8,128)} %seed_ref.3, f32[3,256,128]{2,1,0:T(8,128)} %cou_ref.3, ...), custom_call_target="tpu_custom_call" | custom-call | tf_op jit(solution)/shard_map/pack_sides/pallas_call | solution.py:477
  3.5 3.0 %collective-permute-start = (f32[320,128]{1,0:T(8,128)}, f32[320,128]{1,0:T(8,128)S(1)}, u32[]{:S(2)}, u32[]{:S(2)}) collective-permute-start(f32[320,128]{1,0:T(8,128)} %get-tuple-element.18), channel_id=1, source_target_pairs={{0,1},{1,2},{2,3},{3,0},{4,5},{5,6},{6,7},{7,4},{8,9},{9,10},{10,1... | collective-permute-start | bytes 491528 | tf_op jit(solution)/shard_map/ppermute | solution.py:496
  6.5 1.0 %collective-permute-start.1 = (f32[320,128]{1,0:T(8,128)}, f32[320,128]{1,0:T(8,128)S(1)}, u32[]{:S(2)}, u32[]{:S(2)}) collective-permute-start(f32[320,128]{1,0:T(8,128)} %get-tuple-element.19), channel_id=1, source_target_pairs={{0,3},{1,0},{2,1},{3,2},{4,7},{5,4},{6,5},{7,6},{8,11},{9,8},{10,9... | collective-permute-start | bytes 491528 | tf_op jit(solution)/shard_map/ppermute | solution.py:497
  7.5 5.4 %all-to-all-start = ((f32[32,1,128]{2,1,0:T(1,128)}), f32[32,1,128]{2,1,0:T(1,128)S(1)}, u32[]{:S(2)}, u32[]{:S(2)}) async-start(f32[32,1,128]{2,1,0:T(1,128)} %bitcast.14), calls=%async_computation | async-start | bytes 32768 | tf_op jit(solution)/shard_map/all_to_all | solution.py:498
  12.9 0.0 collective-permute-done.west_ref
  12.9 2.7 %collective-permute-done.1.east_ref = f32[320,128]{1,0:T(8,128)S(1)} collective-permute-done((f32[320,128]{1,0:T(8,128)}, f32[320,128]{1,0:T(8,128)S(1)}, u32[]{:S(2)}, u32[]{:S(2)}) %collective-permute-start.1) | collective-permute-done | bytes 163872 | tf_op jit(solution)/shard_map/ppermute | solution.py:497
  15.6 0.0 copy-done
  15.6 0.0 copy-done.1
  15.6 0.0 copy-done.2
  15.7 0.0 copy-done.3
  15.7 0.1 collective-permute-start.2
  15.8 3.5 %collective-permute-start.3 = (f32[216,128]{1,0:T(8,128)S(1)}, f32[216,128]{1,0:T(8,128)S(1)}, u32[]{:S(2)}, u32[]{:S(2)}) collective-permute-start(f32[216,128]{1,0:T(8,128)S(1)} %get-tuple-element.29), channel_id=1, source_target_pairs={{0,28},{4,0},{8,4},{12,8},{16,12},{20,16},{24,20},{28,24},{1,29},{... | collective-permute-start | bytes 331784 | tf_op jit(solution)/shard_map/ppermute | solution.py:508
  19.3 0.1 pad_add_fusion.place_ref
  19.4 0.7 %all-to-all-done = f32[32,1,128]{2,1,0:T(1,128)S(1)} async-done(((f32[32,1,128]{2,1,0:T(1,128)}), f32[32,1,128]{2,1,0:T(1,128)S(1)}, u32[]{:S(2)}, u32[]{:S(2)}) %all-to-all-start) | async-done | bytes 16416 | tf_op jit(solution)/shard_map/all_to_all | solution.py:498
  20.1 1.5 %prepare.1 = (f32[4,304,128]{2,1,0:T(8,128)S(1)}, f32[4,304,128]{2,1,0:T(8,128)S(1)}, f32[4,304,128]{2,1,0:T(8,128)S(1)}, f32[4,304,128]{2,1,0:T(8,128)S(1)}, f3...) custom-call(s32[2]{0:T(128)S(1)} %pad_add_fusion.place_ref, ...), custom_call_target="tpu_custom_call" | custom-call | flops 40000000 | bytes 8000000 | tf_op jit(solution)/shard_map/prepare/pallas_call | solution.py:512
  21.6 0.2 collective-permute-done.2.low_ref
  21.8 0.0 collective-permute-done.3.high_ref
  21.8 8.9 %window.1 = (f32[3,256,128]{2,1,0:T(8,128)}, f32[32,128]{1,0:T(8,128)S(1)}, f32[4,304,128]{2,1,0:T(8,128)S(1)}, f32[4,304,128]{2,1,0:T(8,128)S(1)}, f32[4,304,12...) custom-call(f32[4,304,128]{2,1,0:T(8,128)S(1)} %get-tuple-element.20, ...), custom_call_target="tpu_custom_call", output_to_operand_aliasing={{2}: (0, {}), {3}: (1, {}), {4}: (2, {}), {5}: (3, {}), {6}... | custom-call | tf_op jit(solution)/shard_map/window/pallas_call | solution.py:526
  30.7 11.7 %all_to_all.20 = f32[32,1,128]{2,1,0:T(1,128)S(1)} all-to-all(f32[32,1,128]{2,1,0:T(1,128)S(1)} %bitcast.13), channel_id=1, replica_groups=mesh['gx'=8,'gy'=4] {'gx','gy'}, dimensions={0} | all-to-all | bytes 32768 | tf_op jit(solution)/shard_map/all_to_all | solution.py:546
  42.4 0.6 %reduce_sum.9 = f32[128]{0:T(128)} reduce(f32[32,1,128]{2,1,0:T(1,128)S(1)} %all_to_all.20, f32[]{:T(128)} %constant.10.clone.1), dimensions={0,1}, to_apply=%region_0.0 | reduce | flops 3968 | bytes 16900 | tf_op jit(solution)/shard_map/reduce_sum | solution.py:547
  (1 shorter events, 0.0 us)
Async XLA Ops:
  0.6 15.0 %copy-start = (f32[3,256,128]{2,1,0:T(8,128)S(1)}, f32[3,256,128]{2,1,0:T(8,128)}, u32[]{:S(2)}) copy-start(f32[3,256,128]{2,1,0:T(8,128)} %vel_ref.3) | copy-start | bytes 1179652
  0.6 15.0 %copy-start.1 = (f32[3,256,128]{2,1,0:T(8,128)S(1)}, f32[3,256,128]{2,1,0:T(8,128)}, u32[]{:S(2)}) copy-start(f32[3,256,128]{2,1,0:T(8,128)} %seed_ref.3) | copy-start | bytes 1179652
  0.7 15.0 %copy-start.2 = (f32[3,256,128]{2,1,0:T(8,128)S(1)}, f32[3,256,128]{2,1,0:T(8,128)}, u32[]{:S(2)}) copy-start(f32[3,256,128]{2,1,0:T(8,128)} %cou_ref.3) | copy-start | bytes 1179652
  0.7 15.0 %copy-start.3 = (f32[3,256,128]{2,1,0:T(8,128)S(1)}, f32[3,256,128]{2,1,0:T(8,128)}, u32[]{:S(2)}) copy-start(f32[3,256,128]{2,1,0:T(8,128)} %vis_ref.3) | copy-start | bytes 1179652
  3.5 9.4 %collective-permute-start = (f32[320,128]{1,0:T(8,128)}, f32[320,128]{1,0:T(8,128)S(1)}, u32[]{:S(2)}, u32[]{:S(2)}) collective-permute-start(f32[320,128]{1,0:T(8,128)} %get-tuple-element.18), channel_id=1, source_target_pairs={{0,1},{1,2},{2,3},{3,0},{4,5},{5,6},{6,7},{7,4},{8,9},{9,10},{10,1... | collective-permute-start | bytes 491528 | tf_op jit(solution)/shard_map/ppermute | solution.py:496
  6.5 9.1 %collective-permute-start.1 = (f32[320,128]{1,0:T(8,128)}, f32[320,128]{1,0:T(8,128)S(1)}, u32[]{:S(2)}, u32[]{:S(2)}) collective-permute-start(f32[320,128]{1,0:T(8,128)} %get-tuple-element.19), channel_id=1, source_target_pairs={{0,3},{1,0},{2,1},{3,2},{4,7},{5,4},{6,5},{7,6},{8,11},{9,8},{10,9... | collective-permute-start | bytes 491528 | tf_op jit(solution)/shard_map/ppermute | solution.py:497
  7.5 12.5 %all-to-all-start = ((f32[32,1,128]{2,1,0:T(1,128)}), f32[32,1,128]{2,1,0:T(1,128)S(1)}, u32[]{:S(2)}, u32[]{:S(2)}) async-start(f32[32,1,128]{2,1,0:T(1,128)} %bitcast.14), calls=%async_computation | async-start | bytes 32768 | tf_op jit(solution)/shard_map/all_to_all | solution.py:498
  15.7 6.1 %collective-permute-start.2 = (f32[216,128]{1,0:T(8,128)S(1)}, f32[216,128]{1,0:T(8,128)S(1)}, u32[]{:S(2)}, u32[]{:S(2)}) collective-permute-start(f32[216,128]{1,0:T(8,128)S(1)} %get-tuple-element.28), channel_id=1, source_target_pairs={{0,4},{4,8},{8,12},{12,16},{16,20},{20,24},{24,28},{28,0},{1,5},{5... | collective-permute-start | bytes 331784 | tf_op jit(solution)/shard_map/ppermute | solution.py:507
  15.8 6.1 %collective-permute-start.3 = (f32[216,128]{1,0:T(8,128)S(1)}, f32[216,128]{1,0:T(8,128)S(1)}, u32[]{:S(2)}, u32[]{:S(2)}) collective-permute-start(f32[216,128]{1,0:T(8,128)S(1)} %get-tuple-element.29), channel_id=1, source_target_pairs={{0,28},{4,0},{8,4},{12,8},{16,12},{20,16},{24,20},{28,24},{1,29},{... | collective-permute-start | bytes 331784 | tf_op jit(solution)/shard_map/ppermute | solution.py:508

commit v3 on v2

--- a/solution.py
+++ b/solution.py
@@ -19,6 +19,7 @@
 MID = 13
 THIN = 8
 GAP = 42
+CENTRE = (CY - GAP, 0, GAP)
 RIM = 16
 TOP = 24
 TALL = CX + 2 * TOP
@@ -44,10 +45,10 @@
 
 
 def rim_place(lane):
-    level = jnp.where((lane >= GAP // 2) & (lane < GAP // 2 + GAP), 1, 0)
-    level = jnp.where((lane >= GAP // 2 + GAP) & (lane < GAP // 2 + 2 * GAP), 2, level)
-    place = lane - GAP * level
-    place = jnp.where(lane >= GAP // 2 + 2 * GAP, lane - CY, place)
+    level = jnp.where((lane >= GAP // 2) & (lane < CY // 2), 2, 1)
+    level = jnp.where((lane >= CY // 2) & (lane < CY - GAP // 2), 0, level)
+    place = lane - jnp.where(level == 2, GAP, jnp.where(level == 0, CY - GAP, 0))
+    place = jnp.where(lane >= CY - GAP // 2, lane - CY, place)
     return level, place
 
 
@@ -113,8 +114,8 @@
         out_ref[CX:SIDE_ROWS, :] = total
 
     def around(ref):
-        value = jnp.where(level_of == 1, rolled(ref[1], GAP), ref[0])
-        return jnp.where(level_of == 2, rolled(ref[2], 2 * GAP), value)
+        value = jnp.where(level_of == 0, rolled(ref[0], -GAP), ref[1])
+        return jnp.where(level_of == 2, rolled(ref[2], GAP), value)
 
     up = down = None
     for index, (ref, width) in enumerate(((vel_ref, WIDE), (cou_ref, MID), (vis_ref, MID))):
@@ -134,7 +135,7 @@
 def in_share(lane, start, width):
     inside = jnp.zeros(lane.shape, jnp.bool_)
     for level in range(LEV):
-        first = GAP * level + start
+        first = CENTRE[level] + start
         inside = inside | ((lane >= first) & (lane < first + width))
     return inside
 
@@ -167,9 +168,9 @@
 def rim_mixes():
     level_of, place = rim_place(lane_ids())
     valid = (place >= -WIDE) & (place < WIDE)
-    from_above = jnp.where(valid & (level_of < LEV - 1), VERTICAL_MIX, 0.0).astype(jnp.float32)
-    from_below = jnp.where(valid & (level_of > 0), VERTICAL_MIX, 0.0).astype(jnp.float32)
-    return valid, from_above, from_below
+    upper = jnp.where(valid & (level_of != 2), VERTICAL_MIX, 0.0).astype(jnp.float32)
+    lower = jnp.where(valid & (level_of != 0), VERTICAL_MIX, 0.0).astype(jnp.float32)
+    return valid, upper, lower
 
 
 def put_coefficients(bufs, tile, to, rows, courant, viscosity, mix):
@@ -181,7 +182,7 @@
 
 def put_rim(u_buf, bufs, west, east, to, rows):
     _, place = rim_place(lane_ids())
-    _, from_above, from_below = rim_mixes()
+    _, upper, lower = rim_mixes()
     zero = jnp.zeros((rows, CY), jnp.float32)
     start = 0
     found = []
@@ -192,14 +193,14 @@
         )
         start += width
     u_buf[LEV, pl.ds(to, rows), :] = found[0]
-    put_coefficients(bufs, LEV, to, rows, found[1], found[2], from_above + from_below)
+    put_coefficients(bufs, LEV, to, rows, found[1], found[2], upper + lower)
 
 
 def put_thin_rim(l_buf, west, east, block, to, rows):
     level_of, place = rim_place(lane_ids())
     value = jnp.zeros((rows, CY), jnp.float32)
     for level in range(LEV):
-        at = GAP * level - (32 * block + THIN * level)
+        at = CENTRE[level] - (32 * block + THIN * level)
         mine = level_of == level
         value = jnp.where(mine & (place >= 0) & (place < THIN), rolled(east, at), value)
         value = jnp.where(mine & (place >= -THIN) & (place < 0), rolled(west, at - THIN), value)
@@ -279,15 +280,15 @@
     per_device,
     u_even_in, l_even_in, a_in, w_in, v_in, d_buf, rows_buf, cols_buf, low_ref, high_ref,
     start_ref, grads_ref, u_even, l_even, a_buf, w_buf, v_buf,
-    u_odd, l_odd, g_buf, f_buf, s_buf,
+    u_odd, l_odd, g_buf, f_buf, s_buf, v_turned,
 ):
     u_buf, l_buf = (u_even, u_odd), (l_even, l_odd)
     bufs = (a_buf, w_buf, v_buf)
     lane = lane_ids()
     level_of, place = rim_place(lane)
     west_lane, east_lane = place == -1, place == 0
-    level_one, level_two = level_of == 1, level_of == 2
-    _, from_above, from_below = rim_mixes()
+    level_zero, level_two = level_of == 0, level_of == 2
+    _, upper, lower = rim_mixes()
     first_lane, last_lane = lane == 0, lane == CY - 1
     devices = grads_ref.shape[0]
 
@@ -315,12 +316,12 @@
         west, east = ref[at : at + THIN, :], ref[at + THIN : at + 2 * THIN, :]
         put_thin_rim(l_even, west, east, block, thin_to, THIN)
 
-    def borders(tiles):
-        packed = tiles[LEV]
-        across = [rolled(packed, -GAP * level) for level in range(LEV)]
-        other = jnp.where(level_one, rolled(tiles[1], GAP), tiles[0])
-        across.append(jnp.where(level_two, rolled(tiles[2], 2 * GAP), other))
-        return across
+    def beyond(packed):
+        return rolled(packed, GAP), rolled(packed, -GAP)
+
+    def outward(tiles):
+        other = jnp.where(level_zero, rolled(tiles[0], -GAP), tiles[1])
+        return jnp.where(level_two, rolled(tiles[2], GAP), other)
 
     def sideways(tiles, across, with_rim=True):
         sums = []
@@ -335,8 +336,11 @@
         middle = VERTICAL_MIX * core[1]
         return [middle, VERTICAL_MIX * (core[0] + core[2]), middle]
 
-    def rim_upright(packed):
-        return from_above * rolled(packed, -GAP) + from_below * rolled(packed, GAP)
+    def rim_upright(plus, minus):
+        return upper * minus + lower * plus
+
+    for index, turned in enumerate(beyond(v_buf[LEV, TOP - 8 : TOP + CX + 8, :])):
+        v_turned[index, TOP - 8 : TOP + CX + 8, :] = turned
 
     def drag_of(tile, at):
         return d_buf[(1, 0, 1, 2)[tile], at, :]
@@ -362,11 +366,13 @@
         now, later = step % 2, (step + 1) % 2
 
         def exchange(at, chunk, _, now=now):
-            return borders([u_buf[now][tile, at, :] for tile in range(LEV + 1)])
-
-        def shift(at, chunk, other, now=now):
             state = [u_buf[now][tile, at, :] for tile in range(LEV + 1)]
-            return sideways(state, other), rim_upright(state[LEV])
+            return *beyond(state[LEV]), outward(state)
+
+        def shift(at, chunk, held, now=now):
+            plus, minus, other = held
+            state = [u_buf[now][tile, at, :] for tile in range(LEV + 1)]
+            return sideways(state, (plus, state[LEV], minus, other)), rim_upright(plus, minus)
 
         def advance(at, chunk, shifted, step=step, now=now, later=later):
             first, rows = chunk
@@ -415,11 +421,14 @@
             return adjoint, [v_buf[tile, at, :] * adjoint[tile] for tile in range(LEV + 1)]
 
         def exchange(at, chunk, _, fluxes=fluxes):
-            return borders(fluxes(at)[1])
-
-        def shift(at, chunk, other, fluxes=fluxes, step=step):
             adjoint, flux = fluxes(at)
-            return sideways(flux, other, bool(step)), rim_upright(adjoint[LEV]) if step else None
+            return *beyond(adjoint[LEV]), outward(flux)
+
+        def shift(at, chunk, held, fluxes=fluxes, step=step):
+            plus, minus, other = held
+            flux = fluxes(at)[1]
+            across = plus * v_turned[0, at, :], flux[LEV], minus * v_turned[1, at, :], other
+            return sideways(flux, across, bool(step)), rim_upright(plus, minus) if step else None
 
         def retreat(at, chunk, shifted, step=step, now=now, later=later):
             first, rows = chunk
@@ -540,6 +549,7 @@
             pltpu.VMEM((STEPS, LEV + 1, TALL, CY), f32),
             pltpu.VMEM((STEPS, LEV, TALL, CY), f32),
             pltpu.VMEM((2, TALL, CY), f32),
+            pltpu.VMEM((2, TALL, CY), f32),
         ],
         compiler_params=pltpu.CompilerParams(vmem_limit_bytes=24 * 1024 * 1024),
     )(*fields, low, high)

time: 43.1 us -> 42.6 us (0.988)
  Pallas kernels: 13.2 us -> 12.7 us
    pallas_call x1, Pallas kernels: 8.86 us -> 8.33 us  [shards(): pl.pallas_call(functools.partial(window, per_device), name='window', out_...]
  transfers between devices with their start and end apart: 5 -> 5, of which waited for: 3 -> 3; matrix products, arithmetic and copies ran while one was open for 0% -> 0% of each run, Pallas kernels for 3% -> 4%
where the time goes in v3:
time: 42.6 us; the launch traced here: 42.4 us
  starting transfers between devices  13 us (31%)
  Pallas kernels  12.7 us (30%)
  blocking collectives  11.7 us (27%)
  waiting for transfers between devices  3.7 us (9%)
  between operations  0.73 us (2%)
  other arithmetic  0.63 us (1%)
    all_to_all x1, blocking collectives, shards(): grads = lax.all_to_all(grads, ('gx', 'gy'), 0, 0, tiled=True)  11.7 us
    pallas_call x1, Pallas kernels, shards(): pl.pallas_call(functools.partial(window, per_device), name='window', out_...  8.33 us
    all_to_all x1, starting transfers between devices, shards(): info = lax.all_to_all(info, ('gx', 'gy'), 0, 0, tiled=True)  5.36 us
    ppermute x1, starting transfers between devices, shards(): high = lax.ppermute(end_down, 'gx', ring('gx', -1))  3.53 us
    ppermute x1, starting transfers between devices, shards(): west = lax.ppermute(side_up, 'gy', ring('gy', 1))  2.99 us
    pallas_call x1, Pallas kernels, shards(): pl.pallas_call(functools.partial(pack_sides, n_gy), name='pack_sides', ou...  2.84 us
    ppermute x1, waiting for transfers between devices, shards(): east = lax.ppermute(side_down, 'gy', ring('gy', -1))  2.72 us
    pallas_call x1, Pallas kernels, shards(): pl.pallas_call(functools.partial(prepare, n_gx, n_gy, per_device), name='...  1.47 us
  transfers between devices with their start and end apart: 5, of which 3 were waited for; matrix products, arithmetic and copies ran while one was open for 0% of the time, Pallas kernels for 4%

profile of v3, /device:TPU:0, one launch (start us, length us, event | category | flops | bytes accessed | tf_op | source)
XLA Modules:
  0.0 42.4 jit_solution(15593545467161001491)
XLA Ops:
  0.6 0.0 copy-start
  0.6 0.0 copy-start.1
  0.7 0.0 copy-start.2
  0.7 0.0 copy-start.3
  0.7 2.8 %pack_sides.1 = (f32[320,128]{1,0:T(8,128)}, f32[320,128]{1,0:T(8,128)}, f32[32,128]{1,0:T(8,128)}) custom-call(s32[4]{0:T(128)} %bitcast.16, s32[2,4]{1,0:T(2,128)} %bitcast.15, f32[4]{0:T(128)} %thrust_hbm.1, f32[4]{0:T(128)} %width_hbm.1, f32[3,256,128]{2,1,0:T(8,128)} %vel_ref.3, f32[3,256,128]{2,1,0:T(8,128)} %seed_ref.3, f32[3,256,128]{2,1,0:T(8,128)} %cou_ref.3, ...), custom_call_target="tpu_custom_call" | custom-call | tf_op jit(solution)/shard_map/pack_sides/pallas_call | solution.py:486
  3.5 3.0 %collective-permute-start = (f32[320,128]{1,0:T(8,128)}, f32[320,128]{1,0:T(8,128)S(1)}, u32[]{:S(2)}, u32[]{:S(2)}) collective-permute-start(f32[320,128]{1,0:T(8,128)} %get-tuple-element.18), channel_id=1, source_target_pairs={{0,1},{1,2},{2,3},{3,0},{4,5},{5,6},{6,7},{7,4},{8,9},{9,10},{10,1... | collective-permute-start | bytes 491528 | tf_op jit(solution)/shard_map/ppermute | solution.py:505
  6.5 1.0 %collective-permute-start.1 = (f32[320,128]{1,0:T(8,128)}, f32[320,128]{1,0:T(8,128)S(1)}, u32[]{:S(2)}, u32[]{:S(2)}) collective-permute-start(f32[320,128]{1,0:T(8,128)} %get-tuple-element.19), channel_id=1, source_target_pairs={{0,3},{1,0},{2,1},{3,2},{4,7},{5,4},{6,5},{7,6},{8,11},{9,8},{10,9... | collective-permute-start | bytes 491528 | tf_op jit(solution)/shard_map/ppermute | solution.py:506
  7.5 5.4 %all-to-all-start = ((f32[32,1,128]{2,1,0:T(1,128)}), f32[32,1,128]{2,1,0:T(1,128)S(1)}, u32[]{:S(2)}, u32[]{:S(2)}) async-start(f32[32,1,128]{2,1,0:T(1,128)} %bitcast.14), calls=%async_computation | async-start | bytes 32768 | tf_op jit(solution)/shard_map/all_to_all | solution.py:507
  12.9 0.0 collective-permute-done.west_ref
  12.9 2.7 %collective-permute-done.1.east_ref = f32[320,128]{1,0:T(8,128)S(1)} collective-permute-done((f32[320,128]{1,0:T(8,128)}, f32[320,128]{1,0:T(8,128)S(1)}, u32[]{:S(2)}, u32[]{:S(2)}) %collective-permute-start.1) | collective-permute-done | bytes 163872 | tf_op jit(solution)/shard_map/ppermute | solution.py:506
  15.6 0.0 copy-done
  15.6 0.0 copy-done.1
  15.6 0.0 copy-done.2
  15.7 0.0 copy-done.3
  15.7 0.1 collective-permute-start.2
  15.8 3.5 %collective-permute-start.3 = (f32[216,128]{1,0:T(8,128)S(1)}, f32[216,128]{1,0:T(8,128)S(1)}, u32[]{:S(2)}, u32[]{:S(2)}) collective-permute-start(f32[216,128]{1,0:T(8,128)S(1)} %get-tuple-element.29), channel_id=1, source_target_pairs={{0,28},{4,0},{8,4},{12,8},{16,12},{20,16},{24,20},{28,24},{1,29},{... | collective-permute-start | bytes 331784 | tf_op jit(solution)/shard_map/ppermute | solution.py:517
  19.3 0.1 pad_add_fusion.place_ref
  19.4 0.7 %all-to-all-done = f32[32,1,128]{2,1,0:T(1,128)S(1)} async-done(((f32[32,1,128]{2,1,0:T(1,128)}), f32[32,1,128]{2,1,0:T(1,128)S(1)}, u32[]{:S(2)}, u32[]{:S(2)}) %all-to-all-start) | async-done | bytes 16416 | tf_op jit(solution)/shard_map/all_to_all | solution.py:507
  20.1 1.5 %prepare.1 = (f32[4,304,128]{2,1,0:T(8,128)S(1)}, f32[4,304,128]{2,1,0:T(8,128)S(1)}, f32[4,304,128]{2,1,0:T(8,128)S(1)}, f32[4,304,128]{2,1,0:T(8,128)S(1)}, f3...) custom-call(s32[2]{0:T(128)S(1)} %pad_add_fusion.place_ref, ...), custom_call_target="tpu_custom_call" | custom-call | flops 40000000 | bytes 8000000 | tf_op jit(solution)/shard_map/prepare/pallas_call | solution.py:521
  21.6 0.3 collective-permute-done.2.low_ref
  21.8 0.0 collective-permute-done.3.high_ref
  21.8 8.3 %window.1 = (f32[3,256,128]{2,1,0:T(8,128)}, f32[32,128]{1,0:T(8,128)S(1)}, f32[4,304,128]{2,1,0:T(8,128)S(1)}, f32[4,304,128]{2,1,0:T(8,128)S(1)}, f32[4,304,12...) custom-call(f32[4,304,128]{2,1,0:T(8,128)S(1)} %get-tuple-element.20, ...), custom_call_target="tpu_custom_call", output_to_operand_aliasing={{2}: (0, {}), {3}: (1, {}), {4}: (2, {}), {5}: (3, {}), {6}... | custom-call | tf_op jit(solution)/shard_map/window/pallas_call | solution.py:535
  30.2 11.7 %all_to_all.20 = f32[32,1,128]{2,1,0:T(1,128)S(1)} all-to-all(f32[32,1,128]{2,1,0:T(1,128)S(1)} %bitcast.13), channel_id=1, replica_groups=mesh['gx'=8,'gy'=4] {'gx','gy'}, dimensions={0} | all-to-all | bytes 32768 | tf_op jit(solution)/shard_map/all_to_all | solution.py:556
  41.9 0.6 %reduce_sum.9 = f32[128]{0:T(128)} reduce(f32[32,1,128]{2,1,0:T(1,128)S(1)} %all_to_all.20, f32[]{:T(128)} %constant.10.clone.1), dimensions={0,1}, to_apply=%region_0.0 | reduce | flops 3968 | bytes 16900 | tf_op jit(solution)/shard_map/reduce_sum | solution.py:557
  (1 shorter events, 0.0 us)
Async XLA Ops:
  0.6 15.0 %copy-start = (f32[3,256,128]{2,1,0:T(8,128)S(1)}, f32[3,256,128]{2,1,0:T(8,128)}, u32[]{:S(2)}) copy-start(f32[3,256,128]{2,1,0:T(8,128)} %vel_ref.3) | copy-start | bytes 1179652
  0.6 15.0 %copy-start.1 = (f32[3,256,128]{2,1,0:T(8,128)S(1)}, f32[3,256,128]{2,1,0:T(8,128)}, u32[]{:S(2)}) copy-start(f32[3,256,128]{2,1,0:T(8,128)} %seed_ref.3) | copy-start | bytes 1179652
  0.7 15.0 %copy-start.2 = (f32[3,256,128]{2,1,0:T(8,128)S(1)}, f32[3,256,128]{2,1,0:T(8,128)}, u32[]{:S(2)}) copy-start(f32[3,256,128]{2,1,0:T(8,128)} %cou_ref.3) | copy-start | bytes 1179652
  0.7 15.0 %copy-start.3 = (f32[3,256,128]{2,1,0:T(8,128)S(1)}, f32[3,256,128]{2,1,0:T(8,128)}, u32[]{:S(2)}) copy-start(f32[3,256,128]{2,1,0:T(8,128)} %vis_ref.3) | copy-start | bytes 1179652
  3.5 9.4 %collective-permute-start = (f32[320,128]{1,0:T(8,128)}, f32[320,128]{1,0:T(8,128)S(1)}, u32[]{:S(2)}, u32[]{:S(2)}) collective-permute-start(f32[320,128]{1,0:T(8,128)} %get-tuple-element.18), channel_id=1, source_target_pairs={{0,1},{1,2},{2,3},{3,0},{4,5},{5,6},{6,7},{7,4},{8,9},{9,10},{10,1... | collective-permute-start | bytes 491528 | tf_op jit(solution)/shard_map/ppermute | solution.py:505
  6.5 9.1 %collective-permute-start.1 = (f32[320,128]{1,0:T(8,128)}, f32[320,128]{1,0:T(8,128)S(1)}, u32[]{:S(2)}, u32[]{:S(2)}) collective-permute-start(f32[320,128]{1,0:T(8,128)} %get-tuple-element.19), channel_id=1, source_target_pairs={{0,3},{1,0},{2,1},{3,2},{4,7},{5,4},{6,5},{7,6},{8,11},{9,8},{10,9... | collective-permute-start | bytes 491528 | tf_op jit(solution)/shard_map/ppermute | solution.py:506
  7.5 12.5 %all-to-all-start = ((f32[32,1,128]{2,1,0:T(1,128)}), f32[32,1,128]{2,1,0:T(1,128)S(1)}, u32[]{:S(2)}, u32[]{:S(2)}) async-start(f32[32,1,128]{2,1,0:T(1,128)} %bitcast.14), calls=%async_computation | async-start | bytes 32768 | tf_op jit(solution)/shard_map/all_to_all | solution.py:507
  15.7 6.1 %collective-permute-start.2 = (f32[216,128]{1,0:T(8,128)S(1)}, f32[216,128]{1,0:T(8,128)S(1)}, u32[]{:S(2)}, u32[]{:S(2)}) collective-permute-start(f32[216,128]{1,0:T(8,128)S(1)} %get-tuple-element.28), channel_id=1, source_target_pairs={{0,4},{4,8},{8,12},{12,16},{16,20},{20,24},{24,28},{28,0},{1,5},{5... | collective-permute-start | bytes 331784 | tf_op jit(solution)/shard_map/ppermute | solution.py:516
  15.8 6.1 %collective-permute-start.3 = (f32[216,128]{1,0:T(8,128)S(1)}, f32[216,128]{1,0:T(8,128)S(1)}, u32[]{:S(2)}, u32[]{:S(2)}) collective-permute-start(f32[216,128]{1,0:T(8,128)S(1)} %get-tuple-element.29), channel_id=1, source_target_pairs={{0,28},{4,0},{8,4},{12,8},{16,12},{20,16},{24,20},{28,24},{1,29},{... | collective-permute-start | bytes 331784 | tf_op jit(solution)/shard_map/ppermute | solution.py:517

commit v4 on v3

--- a/solution.py
+++ b/solution.py
@@ -67,9 +67,18 @@
         body(first + full * chunk, count - full * chunk)
 
 
+def is_odd(axis):
+    return lax.axis_index(axis) % 2 == 1
+
+
+def in_order(axis, first, second):
+    odd = is_odd(axis)
+    return jnp.where(odd, second, first), jnp.where(odd, first, second)
+
+
 def pack_sides(
     n_gy, tile_hbm, offset_hbm, thrust_hbm, width_hbm, vel_hbm, seed_hbm, cou_hbm, vis_hbm,
-    up_ref, down_ref, info_ref,
+    outer_ref, inner_ref, info_ref,
     tile_ref, offset_ref, thrust_ref, width_ref, vel_ref, seed_ref, cou_ref, vis_ref, arrived,
 ):
     copies = [
@@ -101,7 +110,8 @@
     info_ref[...] = jnp.broadcast_to(whole.astype(jnp.float32) + real, info_ref.shape)
 
     copies[0].wait()
-    for out_ref, low in ((up_ref, False), (down_ref, True)):
+    thin = []
+    for low in (True, False):
         total = jnp.zeros((64, CY), jnp.float32)
         for block in range(4):
             for level in range(LEV):
@@ -111,7 +121,8 @@
                     to - (0 if low else CY - THIN),
                 )
                 total = jnp.where((lane >= to) & (lane < to + THIN), moved, total)
-        out_ref[CX:SIDE_ROWS, :] = total
+        thin.append(total)
+    outer_ref[CX:SIDE_ROWS, :], inner_ref[CX:SIDE_ROWS, :] = in_order("gy", *thin)
 
     def around(ref):
         value = jnp.where(level_of == 0, rolled(ref[0], -GAP), ref[1])
@@ -128,8 +139,7 @@
             mine = in_share(lane, start, width)
             up = jnp.where(mine, rolled(both, start + width), up)
             down = jnp.where(mine, rolled(both, start), down)
-    up_ref[0:CX, :] = up
-    down_ref[0:CX, :] = down
+    outer_ref[0:CX, :], inner_ref[0:CX, :] = in_order("gy", down, up)
 
 
 def in_share(lane, start, width):
@@ -140,25 +150,27 @@
     return inside
 
 
-def pack_ends(west_ref, east_ref, vel_ref, seed_ref, cou_ref, vis_ref, up_ref, down_ref):
-    for out_ref, low in ((up_ref, False), (down_ref, True)):
-        at = 0
-        first = 0 if low else CX - RIM
-        for ref in (vel_ref, cou_ref, vis_ref):
-            for level in range(LEV):
-                out_ref[at : at + RIM, :] = ref[level, first : first + RIM, :]
-                at += RIM
-        thin_first = 0 if low else CX - THIN
+def pack_ends(outer_side, inner_side, vel_ref, seed_ref, cou_ref, vis_ref, outer_ref, inner_ref):
+    def put(at, rows, down, up):
+        span = pl.ds(at, rows)
+        outer_ref[span, :], inner_ref[span, :] = in_order("gx", down, up)
+        return at + rows
+
+    at = 0
+    for ref in (vel_ref, cou_ref, vis_ref):
         for level in range(LEV):
-            out_ref[at : at + THIN, :] = seed_ref[level, thin_first : thin_first + THIN, :]
-            at += THIN
-        for ref in (west_ref, east_ref):
-            out_ref[at : at + RIM, :] = ref[first : first + RIM, :]
-            at += RIM
-        side_first = CX if low else SIDE_ROWS - THIN
-        for ref in (west_ref, east_ref):
-            out_ref[at : at + THIN, :] = ref[side_first : side_first + THIN, :]
-            at += THIN
+            at = put(at, RIM, ref[level, 0:RIM, :], ref[level, CX - RIM : CX, :])
+    for level in range(LEV):
+        at = put(at, THIN, seed_ref[level, 0:THIN, :], seed_ref[level, CX - THIN : CX, :])
+    down = in_order("gy", outer_side[0:RIM, :], inner_side[0:RIM, :])
+    up = in_order("gy", outer_side[CX - RIM : CX, :], inner_side[CX - RIM : CX, :])
+    for side in range(2):
+        at = put(at, RIM, down[side], up[side])
+    last = SIDE_ROWS - THIN
+    down = in_order("gy", outer_side[CX : CX + THIN, :], inner_side[CX : CX + THIN, :])
+    up = in_order("gy", outer_side[last:SIDE_ROWS, :], inner_side[last:SIDE_ROWS, :])
+    for side in range(2):
+        at = put(at, THIN, down[side], up[side])
 
 
 def level_mix(level):
@@ -209,7 +221,7 @@
 
 def prepare(
     n_gx, n_gy, per_device,
-    place_ref, info_ref, vel_ref, seed_ref, cou_ref, vis_ref, west_ref, east_ref,
+    place_ref, info_ref, vel_ref, seed_ref, cou_ref, vis_ref, outer_side, inner_side,
     u_buf, l_buf, a_buf, w_buf, v_buf, d_buf, rows_buf, cols_buf,
 ):
     lane = lane_ids()
@@ -270,15 +282,15 @@
         u_buf[level, inside, :] = vel_ref[level]
         l_buf[level, inside, :] = seed_ref[level]
         put_coefficients(bufs, level, TOP, CX, cou_ref[level], vis_ref[level], level_mix(level))
-    put_rim(u_buf, bufs, west_ref[0:CX, :], east_ref[0:CX, :], TOP, CX)
+    west, east = in_order("gy", outer_side[...], inner_side[...])
+    put_rim(u_buf, bufs, west[0:CX], east[0:CX], TOP, CX)
     for block in range(4):
-        at = pl.ds(CX, 64)
-        put_thin_rim(l_buf, west_ref[at, :], east_ref[at, :], block, TOP + 64 * block, 64)
+        put_thin_rim(l_buf, west[CX:], east[CX:], block, TOP + 64 * block, 64)
 
 
 def window(
     per_device,
-    u_even_in, l_even_in, a_in, w_in, v_in, d_buf, rows_buf, cols_buf, low_ref, high_ref,
+    u_even_in, l_even_in, a_in, w_in, v_in, d_buf, rows_buf, cols_buf, outer_end, inner_end,
     start_ref, grads_ref, u_even, l_even, a_buf, w_buf, v_buf,
     u_odd, l_odd, g_buf, f_buf, s_buf, v_turned,
 ):
@@ -299,21 +311,22 @@
             buf[tile, TALL - TOP + RIM :, :] = edge
         l_odd[tile, TOP - RIM : TOP - THIN, :] = edge
         l_odd[tile, TOP + CX + THIN : TOP + CX + RIM, :] = edge
+    low_end, high_end = in_order("gx", outer_end[...], inner_end[...])
     for ref, to, thin_to, block in (
-        (low_ref, TOP - RIM, TOP - THIN, 3),
-        (high_ref, TOP + CX, TOP + CX, 0),
+        (low_end, TOP - RIM, TOP - THIN, 3),
+        (high_end, TOP + CX, TOP + CX, 0),
     ):
         for level in range(LEV):
-            u_even[level, to : to + RIM, :] = ref[RIM * level : RIM * level + RIM, :]
-            courant = ref[RIM * (LEV + level) : RIM * (LEV + level) + RIM, :]
-            viscosity = ref[RIM * (2 * LEV + level) : RIM * (2 * LEV + level) + RIM, :]
+            u_even[level, to : to + RIM, :] = ref[RIM * level : RIM * level + RIM]
+            courant = ref[RIM * (LEV + level) : RIM * (LEV + level) + RIM]
+            viscosity = ref[RIM * (2 * LEV + level) : RIM * (2 * LEV + level) + RIM]
             put_coefficients(bufs, level, to, RIM, courant, viscosity, level_mix(level))
             at = 3 * LEV * RIM + THIN * level
-            l_even[level, thin_to : thin_to + THIN, :] = ref[at : at + THIN, :]
+            l_even[level, thin_to : thin_to + THIN, :] = ref[at : at + THIN]
         at = 3 * LEV * RIM + LEV * THIN
-        put_rim(u_even, bufs, ref[at : at + RIM, :], ref[at + RIM : at + 2 * RIM, :], to, RIM)
+        put_rim(u_even, bufs, ref[at : at + RIM], ref[at + RIM : at + 2 * RIM], to, RIM)
         at += 2 * RIM
-        west, east = ref[at : at + THIN, :], ref[at + THIN : at + 2 * THIN, :]
+        west, east = ref[at : at + THIN], ref[at + THIN : at + 2 * THIN]
         put_thin_rim(l_even, west, east, block, thin_to, THIN)
 
     def beyond(packed):
@@ -476,14 +489,16 @@
     devices = n_gx * n_gy
     per_device = thrust.shape[0]
     f32 = jnp.float32
-    smem = pl.BlockSpec(memory_space=pltpu.SMEM)
     vmem = pl.BlockSpec(memory_space=pltpu.VMEM)
 
-    def ring(axis, by):
+    def swap(axis, array, odd_up):
         count = lax.axis_size(axis)
-        return [(i, (i + by) % count) for i in range(count)]
-
-    side_up, side_down, info = pl.pallas_call(
+        step = 1 if odd_up else -1
+        return lax.ppermute(
+            array, axis, [(i, (i + (step if i % 2 else -step)) % count) for i in range(count)]
+        )
+
+    outer, inner, info = pl.pallas_call(
         functools.partial(pack_sides, n_gy),
         name="pack_sides",
         out_shape=(
@@ -502,19 +517,17 @@
             pltpu.SemaphoreType.DMA((8,)),
         ],
     )(turbine_tile.reshape(per_device), turbine_offset.T, thrust, disk_width, velocity, adjoint_seed, courant, viscosity)
-    west = lax.ppermute(side_up, "gy", ring("gy", 1))
-    east = lax.ppermute(side_down, "gy", ring("gy", -1))
+    outer_side, inner_side = swap("gy", outer, True), swap("gy", inner, False)
     info = lax.all_to_all(info, ("gx", "gy"), 0, 0, tiled=True)
-    end_up, end_down = pl.pallas_call(
+    outer, inner = pl.pallas_call(
         pack_ends,
         name="pack_ends",
         out_shape=(jax.ShapeDtypeStruct((END_ROWS, CY), f32),) * 2,
         in_specs=[vmem] * 6,
         out_specs=(vmem,) * 2,
         compiler_params=SMALL,
-    )(west, east, velocity, adjoint_seed, courant, viscosity)
-    low = lax.ppermute(end_up, "gx", ring("gx", 1))
-    high = lax.ppermute(end_down, "gx", ring("gx", -1))
+    )(outer_side, inner_side, velocity, adjoint_seed, courant, viscosity)
+    outer_end, inner_end = swap("gx", outer, True), swap("gx", inner, False)
     place = jnp.stack([lax.axis_index("gx"), lax.axis_index("gy")]).astype(jnp.int32)
     turbines = devices * per_device
     field = jax.ShapeDtypeStruct((LEV + 1, TALL, CY), f32)
@@ -527,11 +540,11 @@
             jax.ShapeDtypeStruct((turbines, CX), f32),
             jax.ShapeDtypeStruct((turbines, CY), f32),
         ),
-        in_specs=[smem] + [vmem] * 7,
+        in_specs=[pl.BlockSpec(memory_space=pltpu.SMEM)] + [vmem] * 7,
         out_specs=(vmem,) * 8,
         compiler_params=SMALL,
         cost_estimate=pl.CostEstimate(flops=40000000, bytes_accessed=8000000, transcendentals=0),
-    )(place, info, velocity, adjoint_seed, courant, viscosity, west, east)
+    )(place, info, velocity, adjoint_seed, courant, viscosity, outer_side, inner_side)
     adjoint_start, grads, *_ = pl.pallas_call(
         functools.partial(window, per_device),
         name="window",
@@ -552,7 +565,7 @@
             pltpu.VMEM((2, TALL, CY), f32),
         ],
         compiler_params=pltpu.CompilerParams(vmem_limit_bytes=24 * 1024 * 1024),
-    )(*fields, low, high)
+    )(*fields, outer_end, inner_end)
     grads = lax.all_to_all(grads, ("gx", "gy"), 0, 0, tiled=True)
     return adjoint_start, jnp.sum(grads, axis=0)[:per_device]
 

time: 42.6 us -> 42.4 us (level)
  waiting for transfers between devices: 3.7 us -> 5.77 us
  starting transfers between devices: 13 us -> 11.6 us
  blocking collectives: 11.7 us -> 10.6 us
    all_to_all x1, waiting for transfers between devices: 0.72 us -> 2.06 us  [shards(): info = lax.all_to_all(info, ('gx', 'gy'), 0, 0, tiled=True)]
    all_to_all x1, blocking collectives: 11.7 us -> 10.6 us  [shards(): grads = lax.all_to_all(grads, ('gx', 'gy'), 0, 0, tiled=True)]
    ppermute x4, starting transfers between devices: 7.6 us -> 6.73 us  [swap(): lax.ppermute(array, axis, [(i, (i + (step if i % 2 else -step)) % count)...]
    ppermute x4, waiting for transfers between devices: 2.98 us -> 3.71 us  [swap(): lax.ppermute(array, axis, [(i, (i + (step if i % 2 else -step)) % count)...]
    all_to_all x1, starting transfers between devices: 5.36 us -> 4.89 us  [shards(): info = lax.all_to_all(info, ('gx', 'gy'), 0, 0, tiled=True)]
where the time goes in v4:
time: 42.4 us; the launch traced here: 42.2 us
  Pallas kernels  12.8 us (30%)
  starting transfers between devices  11.6 us (27%)
  blocking collectives  10.6 us (25%)
  waiting for transfers between devices  5.77 us (14%)
  between operations  0.73 us (2%)
  other arithmetic  0.63 us (1%)
    all_to_all x1, blocking collectives, shards(): grads = lax.all_to_all(grads, ('gx', 'gy'), 0, 0, tiled=True)  10.6 us
    pallas_call x1, Pallas kernels, shards(): pl.pallas_call(functools.partial(window, per_device), name='window', out_...  8.47 us
    ppermute x4, starting transfers between devices, swap(): lax.ppermute(array, axis, [(i, (i + (step if i % 2 else -step)) % count)...  6.73 us
    all_to_all x1, starting transfers between devices, shards(): info = lax.all_to_all(info, ('gx', 'gy'), 0, 0, tiled=True)  4.89 us
    ppermute x4, waiting for transfers between devices, swap(): lax.ppermute(array, axis, [(i, (i + (step if i % 2 else -step)) % count)...  3.71 us
    pallas_call x1, Pallas kernels, shards(): pl.pallas_call(functools.partial(pack_sides, n_gy), name='pack_sides', ou...  2.84 us
    all_to_all x1, waiting for transfers between devices, shards(): info = lax.all_to_all(info, ('gx', 'gy'), 0, 0, tiled=True)  2.06 us
    pallas_call x1, Pallas kernels, shards(): pl.pallas_call(functools.partial(prepare, n_gx, n_gy, per_device), name='...  1.49 us
  transfers between devices with their start and end apart: 5, of which 3 were waited for; matrix products, arithmetic and copies ran while one was open for 0% of the time, Pallas kernels for 4%

profile of v4, /device:TPU:0, one launch (start us, length us, event | category | flops | bytes accessed | tf_op | source)
XLA Modules:
  0.0 42.2 jit_solution(11237308020314435318)
XLA Ops:
  0.6 0.0 copy-start
  0.6 0.0 copy-start.1
  0.7 0.0 copy-start.2
  0.7 0.0 copy-start.3
  0.7 2.8 %pack_sides.1 = (f32[320,128]{1,0:T(8,128)}, f32[320,128]{1,0:T(8,128)}, f32[32,128]{1,0:T(8,128)}) custom-call(s32[4]{0:T(128)} %bitcast.16, s32[2,4]{1,0:T(2,128)} %bitcast.15, f32[4]{0:T(128)} %thrust_hbm.1, f32[4]{0:T(128)} %width_hbm.1, f32[3,256,128]{2,1,0:T(8,128)} %vel_ref.3, f32[3,256,128]{2,1,0:T(8,128)} %seed_ref.3, f32[3,256,128]{2,1,0:T(8,128)} %cou_ref.3, ...), custom_call_target="tpu_custom_call" | custom-call | tf_op jit(solution)/shard_map/pack_sides/pallas_call | solution.py:501
  3.5 4.0 %collective-permute-start = (f32[320,128]{1,0:T(8,128)}, f32[320,128]{1,0:T(8,128)S(1)}, u32[]{:S(2)}, u32[]{:S(2)}) collective-permute-start(f32[320,128]{1,0:T(8,128)} %get-tuple-element.18), channel_id=1, source_target_pairs={{0,3},{1,2},{2,1},{3,0},{4,7},{5,6},{6,5},{7,4},{8,11},{9,10},{10,... | collective-permute-start | bytes 491528 | tf_op jit(solution)/shard_map/ppermute | solution.py:497
  7.5 0.5 %collective-permute-start.1 = (f32[320,128]{1,0:T(8,128)}, f32[320,128]{1,0:T(8,128)S(1)}, u32[]{:S(2)}, u32[]{:S(2)}) collective-permute-start(f32[320,128]{1,0:T(8,128)} %get-tuple-element.19), channel_id=1, source_target_pairs={{0,1},{1,0},{2,3},{3,2},{4,5},{5,4},{6,7},{7,6},{8,9},{9,8},{10,11... | collective-permute-start | bytes 491528 | tf_op jit(solution)/shard_map/ppermute | solution.py:497
  8.0 4.9 %all-to-all-start = ((f32[32,1,128]{2,1,0:T(1,128)}), f32[32,1,128]{2,1,0:T(1,128)S(1)}, u32[]{:S(2)}, u32[]{:S(2)}) async-start(f32[32,1,128]{2,1,0:T(1,128)} %bitcast.14), calls=%async_computation | async-start | bytes 32768 | tf_op jit(solution)/shard_map/all_to_all | solution.py:521
  12.9 0.0 collective-permute-done.outer_side
  12.9 2.7 %collective-permute-done.1.inner_side = f32[320,128]{1,0:T(8,128)S(1)} collective-permute-done((f32[320,128]{1,0:T(8,128)}, f32[320,128]{1,0:T(8,128)S(1)}, u32[]{:S(2)}, u32[]{:S(2)}) %collective-permute-start.1) | collective-permute-done | bytes 163872 | tf_op jit(solution)/shard_map/ppermute | solution.py:497
  15.6 0.0 copy-done
  15.7 0.0 copy-done.1
  15.7 0.0 copy-done.2
  15.7 0.0 copy-done.3
  15.7 2.2 %collective-permute-start.2 = (f32[216,128]{1,0:T(8,128)S(1)}, f32[216,128]{1,0:T(8,128)S(1)}, u32[]{:S(2)}, u32[]{:S(2)}) collective-permute-start(f32[216,128]{1,0:T(8,128)S(1)} %get-tuple-element.28), channel_id=1, source_target_pairs={{0,28},{4,8},{8,4},{12,16},{16,12},{20,24},{24,20},{28,0},{1,29},{... | collective-permute-start | bytes 331784 | tf_op jit(solution)/shard_map/ppermute | solution.py:497
  17.9 0.0 collective-permute-start.3
  18.0 0.1 pad_add_fusion.place_ref
  18.0 2.1 %all-to-all-done = f32[32,1,128]{2,1,0:T(1,128)S(1)} async-done(((f32[32,1,128]{2,1,0:T(1,128)}), f32[32,1,128]{2,1,0:T(1,128)S(1)}, u32[]{:S(2)}, u32[]{:S(2)}) %all-to-all-start) | async-done | bytes 16416 | tf_op jit(solution)/shard_map/all_to_all | solution.py:521
  20.1 1.5 %prepare.1 = (f32[4,304,128]{2,1,0:T(8,128)S(1)}, f32[4,304,128]{2,1,0:T(8,128)S(1)}, f32[4,304,128]{2,1,0:T(8,128)S(1)}, f32[4,304,128]{2,1,0:T(8,128)S(1)}, f3...) custom-call(s32[2]{0:T(128)S(1)} %pad_add_fusion.place_ref, ...), custom_call_target="tpu_custom_call" | custom-call | flops 40000000 | bytes 8000000 | tf_op jit(solution)/shard_map/prepare/pallas_call | solution.py:534
  21.6 1.0 %collective-permute-done.2.outer_end = f32[216,128]{1,0:T(8,128)S(1)} collective-permute-done((f32[216,128]{1,0:T(8,128)S(1)}, f32[216,128]{1,0:T(8,128)S(1)}, u32[]{:S(2)}, u32[]{:S(2)}) %collective-permute-start.2) | collective-permute-done | bytes 110624 | tf_op jit(solution)/shard_map/ppermute | solution.py:497
  22.6 0.0 collective-permute-done.3.inner_end
  22.6 8.5 %window.1 = (f32[3,256,128]{2,1,0:T(8,128)}, f32[32,128]{1,0:T(8,128)S(1)}, f32[4,304,128]{2,1,0:T(8,128)S(1)}, f32[4,304,128]{2,1,0:T(8,128)S(1)}, f32[4,304,12...) custom-call(f32[4,304,128]{2,1,0:T(8,128)S(1)} %get-tuple-element.20, ...), custom_call_target="tpu_custom_call", output_to_operand_aliasing={{2}: (0, {}), {3}: (1, {}), {4}: (2, {}), {5}: (3, {}), {6}... | custom-call | tf_op jit(solution)/shard_map/window/pallas_call | solution.py:548
  31.0 10.6 %all_to_all.20 = f32[32,1,128]{2,1,0:T(1,128)S(1)} all-to-all(f32[32,1,128]{2,1,0:T(1,128)S(1)} %bitcast.13), channel_id=1, replica_groups=mesh['gx'=8,'gy'=4] {'gx','gy'}, dimensions={0} | all-to-all | bytes 32768 | tf_op jit(solution)/shard_map/all_to_all | solution.py:569
  41.6 0.6 %reduce_sum.9 = f32[128]{0:T(128)} reduce(f32[32,1,128]{2,1,0:T(1,128)S(1)} %all_to_all.20, f32[]{:T(128)} %constant.10.clone.1), dimensions={0,1}, to_apply=%region_0.0 | reduce | flops 3968 | bytes 16900 | tf_op jit(solution)/shard_map/reduce_sum | solution.py:570
  (1 shorter events, 0.0 us)
Async XLA Ops:
  0.6 15.0 %copy-start = (f32[3,256,128]{2,1,0:T(8,128)S(1)}, f32[3,256,128]{2,1,0:T(8,128)}, u32[]{:S(2)}) copy-start(f32[3,256,128]{2,1,0:T(8,128)} %vel_ref.3) | copy-start | bytes 1179652
  0.6 15.0 %copy-start.1 = (f32[3,256,128]{2,1,0:T(8,128)S(1)}, f32[3,256,128]{2,1,0:T(8,128)}, u32[]{:S(2)}) copy-start(f32[3,256,128]{2,1,0:T(8,128)} %seed_ref.3) | copy-start | bytes 1179652
  0.7 15.0 %copy-start.2 = (f32[3,256,128]{2,1,0:T(8,128)S(1)}, f32[3,256,128]{2,1,0:T(8,128)}, u32[]{:S(2)}) copy-start(f32[3,256,128]{2,1,0:T(8,128)} %cou_ref.3) | copy-start | bytes 1179652
  0.7 15.0 %copy-start.3 = (f32[3,256,128]{2,1,0:T(8,128)S(1)}, f32[3,256,128]{2,1,0:T(8,128)}, u32[]{:S(2)}) copy-start(f32[3,256,128]{2,1,0:T(8,128)} %vis_ref.3) | copy-start | bytes 1179652
  3.5 9.4 %collective-permute-start = (f32[320,128]{1,0:T(8,128)}, f32[320,128]{1,0:T(8,128)S(1)}, u32[]{:S(2)}, u32[]{:S(2)}) collective-permute-start(f32[320,128]{1,0:T(8,128)} %get-tuple-element.18), channel_id=1, source_target_pairs={{0,3},{1,2},{2,1},{3,0},{4,7},{5,6},{6,5},{7,4},{8,11},{9,10},{10,... | collective-permute-start | bytes 491528 | tf_op jit(solution)/shard_map/ppermute | solution.py:497
  7.5 8.2 %collective-permute-start.1 = (f32[320,128]{1,0:T(8,128)}, f32[320,128]{1,0:T(8,128)S(1)}, u32[]{:S(2)}, u32[]{:S(2)}) collective-permute-start(f32[320,128]{1,0:T(8,128)} %get-tuple-element.19), channel_id=1, source_target_pairs={{0,1},{1,0},{2,3},{3,2},{4,5},{5,4},{6,7},{7,6},{8,9},{9,8},{10,11... | collective-permute-start | bytes 491528 | tf_op jit(solution)/shard_map/ppermute | solution.py:497
  8.0 12.1 %all-to-all-start = ((f32[32,1,128]{2,1,0:T(1,128)}), f32[32,1,128]{2,1,0:T(1,128)S(1)}, u32[]{:S(2)}, u32[]{:S(2)}) async-start(f32[32,1,128]{2,1,0:T(1,128)} %bitcast.14), calls=%async_computation | async-start | bytes 32768 | tf_op jit(solution)/shard_map/all_to_all | solution.py:521
  15.7 6.9 %collective-permute-start.2 = (f32[216,128]{1,0:T(8,128)S(1)}, f32[216,128]{1,0:T(8,128)S(1)}, u32[]{:S(2)}, u32[]{:S(2)}) collective-permute-start(f32[216,128]{1,0:T(8,128)S(1)} %get-tuple-element.28), channel_id=1, source_target_pairs={{0,28},{4,8},{8,4},{12,16},{16,12},{20,24},{24,20},{28,0},{1,29},{... | collective-permute-start | bytes 331784 | tf_op jit(solution)/shard_map/ppermute | solution.py:497
  17.9 4.6 %collective-permute-start.3 = (f32[216,128]{1,0:T(8,128)S(1)}, f32[216,128]{1,0:T(8,128)S(1)}, u32[]{:S(2)}, u32[]{:S(2)}) collective-permute-start(f32[216,128]{1,0:T(8,128)S(1)} %get-tuple-element.29), channel_id=1, source_target_pairs={{0,4},{4,0},{8,12},{12,8},{16,20},{20,16},{24,28},{28,24},{1,5},{5... | collective-permute-start | bytes 331784 | tf_op jit(solution)/shard_map/ppermute | solution.py:497

commit v5 on v4

--- a/solution.py
+++ b/solution.py
@@ -292,7 +292,7 @@
     per_device,
     u_even_in, l_even_in, a_in, w_in, v_in, d_buf, rows_buf, cols_buf, outer_end, inner_end,
     start_ref, grads_ref, u_even, l_even, a_buf, w_buf, v_buf,
-    u_odd, l_odd, g_buf, f_buf, s_buf, v_turned,
+    u_odd, l_odd, g_buf, f_buf, s_buf, v_turned, turns,
 ):
     u_buf, l_buf = (u_even, u_odd), (l_even, l_odd)
     bufs = (a_buf, w_buf, v_buf)
@@ -330,7 +330,23 @@
         put_thin_rim(l_even, west, east, block, thin_to, THIN)
 
     def beyond(packed):
-        return rolled(packed, GAP), rolled(packed, -GAP)
+        high = packed.astype(jnp.bfloat16)
+        low = (packed - high.astype(jnp.float32)).astype(jnp.bfloat16)
+        both = lax.dot_general(
+            jnp.concatenate([high, low], axis=1), turns[...], (((1,), (0,)), ((), ())),
+            preferred_element_type=jnp.float32,
+        )
+        return both[:, :CY], both[:, CY:]
+
+    def whole_turned(buf, rows_beyond):
+        first = TOP - rows_beyond
+        plus, minus = beyond(buf[LEV, first : TOP + CX + rows_beyond, :])
+        return first, plus, minus
+
+    def cut(turned, chunk):
+        first, plus, minus = turned
+        at, rows = chunk[0] - first, chunk[1]
+        return plus[at : at + rows], minus[at : at + rows]
 
     def outward(tiles):
         other = jnp.where(level_zero, rolled(tiles[0], -GAP), tiles[1])
@@ -352,7 +368,12 @@
     def rim_upright(plus, minus):
         return upper * minus + lower * plus
 
-    for index, turned in enumerate(beyond(v_buf[LEV, TOP - 8 : TOP + CX + 8, :])):
+    source = lax.broadcasted_iota(jnp.int32, (2 * CY, 2 * CY), 0) % CY
+    target = lax.broadcasted_iota(jnp.int32, (2 * CY, 2 * CY), 1)
+    wanted = (target % CY + jnp.where(target < CY, CY - GAP, GAP)) % CY
+    turns[...] = jnp.where(source == wanted, 1.0, 0.0).astype(jnp.bfloat16)
+    rim_spread = v_buf[LEV, TOP - 8 : TOP + CX + 8, :]
+    for index, turned in enumerate((rolled(rim_spread, GAP), rolled(rim_spread, -GAP))):
         v_turned[index, TOP - 8 : TOP + CX + 8, :] = turned
 
     def drag_of(tile, at):
@@ -378,9 +399,11 @@
         rows_beyond = RIM if STEPS + 5 - step > 8 else 8
         now, later = step % 2, (step + 1) % 2
 
-        def exchange(at, chunk, _, now=now):
+        turned = whole_turned(u_buf[now], rows_beyond)
+
+        def exchange(at, chunk, _, now=now, turned=turned):
             state = [u_buf[now][tile, at, :] for tile in range(LEV + 1)]
-            return *beyond(state[LEV]), outward(state)
+            return *cut(turned, chunk), outward(state)
 
         def shift(at, chunk, held, now=now):
             plus, minus, other = held
@@ -433,9 +456,10 @@
             adjoint = [l_buf[now][tile, at, :] for tile in range(LEV + 1)]
             return adjoint, [v_buf[tile, at, :] * adjoint[tile] for tile in range(LEV + 1)]
 
-        def exchange(at, chunk, _, fluxes=fluxes):
-            adjoint, flux = fluxes(at)
-            return *beyond(adjoint[LEV]), outward(flux)
+        turned = whole_turned(l_buf[now], rows_beyond)
+
+        def exchange(at, chunk, _, fluxes=fluxes, turned=turned):
+            return *cut(turned, chunk), outward(fluxes(at)[1])
 
         def shift(at, chunk, held, fluxes=fluxes, step=step):
             plus, minus, other = held
@@ -563,6 +587,7 @@
             pltpu.VMEM((STEPS, LEV, TALL, CY), f32),
             pltpu.VMEM((2, TALL, CY), f32),
             pltpu.VMEM((2, TALL, CY), f32),
+            pltpu.VMEM((2 * CY, 2 * CY), jnp.bfloat16),
         ],
         compiler_params=pltpu.CompilerParams(vmem_limit_bytes=24 * 1024 * 1024),
     )(*fields, outer_end, inner_end)

time: 42.4 us -> 42.1 us (level)
  no operation moved by 1% of the time
where the time goes in v5:
time: 42.1 us; the launch traced here: 41.9 us
  Pallas kernels  12.5 us (30%)
  starting transfers between devices  11.6 us (28%)
  blocking collectives  10.6 us (25%)
  waiting for transfers between devices  5.77 us (14%)
  between operations  0.73 us (2%)
  other arithmetic  0.63 us (1%)
    all_to_all x1, blocking collectives, shards(): grads = lax.all_to_all(grads, ('gx', 'gy'), 0, 0, tiled=True)  10.6 us
    pallas_call x1, Pallas kernels, shards(): pl.pallas_call(functools.partial(window, per_device), name='window', out_...  8.15 us
    ppermute x4, starting transfers between devices, swap(): lax.ppermute(array, axis, [(i, (i + (step if i % 2 else -step)) % count)...  6.73 us
    all_to_all x1, starting transfers between devices, shards(): info = lax.all_to_all(info, ('gx', 'gy'), 0, 0, tiled=True)  4.89 us
    ppermute x4, waiting for transfers between devices, swap(): lax.ppermute(array, axis, [(i, (i + (step if i % 2 else -step)) % count)...  3.71 us
    pallas_call x1, Pallas kernels, shards(): pl.pallas_call(functools.partial(pack_sides, n_gy), name='pack_sides', ou...  2.84 us
    all_to_all x1, waiting for transfers between devices, shards(): info = lax.all_to_all(info, ('gx', 'gy'), 0, 0, tiled=True)  2.06 us
    pallas_call x1, Pallas kernels, shards(): pl.pallas_call(functools.partial(prepare, n_gx, n_gy, per_device), name='...  1.49 us
  transfers between devices with their start and end apart: 5, of which 3 were waited for; matrix products, arithmetic and copies ran while one was open for 0% of the time, Pallas kernels for 4%

profile of v5, /device:TPU:0, one launch (start us, length us, event | category | flops | bytes accessed | tf_op | source)
XLA Modules:
  0.0 41.9 jit_solution(2755248031785230932)
XLA Ops:
  0.6 0.0 copy-start
  0.6 0.0 copy-start.1
  0.7 0.0 copy-start.2
  0.7 0.0 copy-start.3
  0.7 2.8 %pack_sides.1 = (f32[320,128]{1,0:T(8,128)}, f32[320,128]{1,0:T(8,128)}, f32[32,128]{1,0:T(8,128)}) custom-call(s32[4]{0:T(128)} %bitcast.16, s32[2,4]{1,0:T(2,128)} %bitcast.15, f32[4]{0:T(128)} %thrust_hbm.1, f32[4]{0:T(128)} %width_hbm.1, f32[3,256,128]{2,1,0:T(8,128)} %vel_ref.3, f32[3,256,128]{2,1,0:T(8,128)} %seed_ref.3, f32[3,256,128]{2,1,0:T(8,128)} %cou_ref.3, ...), custom_call_target="tpu_custom_call" | custom-call | tf_op jit(solution)/shard_map/pack_sides/pallas_call | solution.py:525
  3.5 4.0 %collective-permute-start = (f32[320,128]{1,0:T(8,128)}, f32[320,128]{1,0:T(8,128)S(1)}, u32[]{:S(2)}, u32[]{:S(2)}) collective-permute-start(f32[320,128]{1,0:T(8,128)} %get-tuple-element.18), channel_id=1, source_target_pairs={{0,3},{1,2},{2,1},{3,0},{4,7},{5,6},{6,5},{7,4},{8,11},{9,10},{10,... | collective-permute-start | bytes 491528 | tf_op jit(solution)/shard_map/ppermute | solution.py:521
  7.5 0.5 %collective-permute-start.1 = (f32[320,128]{1,0:T(8,128)}, f32[320,128]{1,0:T(8,128)S(1)}, u32[]{:S(2)}, u32[]{:S(2)}) collective-permute-start(f32[320,128]{1,0:T(8,128)} %get-tuple-element.19), channel_id=1, source_target_pairs={{0,1},{1,0},{2,3},{3,2},{4,5},{5,4},{6,7},{7,6},{8,9},{9,8},{10,11... | collective-permute-start | bytes 491528 | tf_op jit(solution)/shard_map/ppermute | solution.py:521
  8.0 4.9 %all-to-all-start = ((f32[32,1,128]{2,1,0:T(1,128)}), f32[32,1,128]{2,1,0:T(1,128)S(1)}, u32[]{:S(2)}, u32[]{:S(2)}) async-start(f32[32,1,128]{2,1,0:T(1,128)} %bitcast.14), calls=%async_computation | async-start | bytes 32768 | tf_op jit(solution)/shard_map/all_to_all | solution.py:545
  12.9 0.0 collective-permute-done.outer_side
  12.9 2.7 %collective-permute-done.1.inner_side = f32[320,128]{1,0:T(8,128)S(1)} collective-permute-done((f32[320,128]{1,0:T(8,128)}, f32[320,128]{1,0:T(8,128)S(1)}, u32[]{:S(2)}, u32[]{:S(2)}) %collective-permute-start.1) | collective-permute-done | bytes 163872 | tf_op jit(solution)/shard_map/ppermute | solution.py:521
  15.6 0.0 copy-done
  15.7 0.0 copy-done.1
  15.7 0.0 copy-done.2
  15.7 0.0 copy-done.3
  15.7 2.2 %collective-permute-start.2 = (f32[216,128]{1,0:T(8,128)S(1)}, f32[216,128]{1,0:T(8,128)S(1)}, u32[]{:S(2)}, u32[]{:S(2)}) collective-permute-start(f32[216,128]{1,0:T(8,128)S(1)} %get-tuple-element.28), channel_id=1, source_target_pairs={{0,28},{4,8},{8,4},{12,16},{16,12},{20,24},{24,20},{28,0},{1,29},{... | collective-permute-start | bytes 331784 | tf_op jit(solution)/shard_map/ppermute | solution.py:521
  17.9 0.0 collective-permute-start.3
  18.0 0.1 pad_add_fusion.place_ref
  18.0 2.1 %all-to-all-done = f32[32,1,128]{2,1,0:T(1,128)S(1)} async-done(((f32[32,1,128]{2,1,0:T(1,128)}), f32[32,1,128]{2,1,0:T(1,128)S(1)}, u32[]{:S(2)}, u32[]{:S(2)}) %all-to-all-start) | async-done | bytes 16416 | tf_op jit(solution)/shard_map/all_to_all | solution.py:545
  20.1 1.5 %prepare.1 = (f32[4,304,128]{2,1,0:T(8,128)S(1)}, f32[4,304,128]{2,1,0:T(8,128)S(1)}, f32[4,304,128]{2,1,0:T(8,128)S(1)}, f32[4,304,128]{2,1,0:T(8,128)S(1)}, f3...) custom-call(s32[2]{0:T(128)S(1)} %pad_add_fusion.place_ref, ...), custom_call_target="tpu_custom_call" | custom-call | flops 40000000 | bytes 8000000 | tf_op jit(solution)/shard_map/prepare/pallas_call | solution.py:558
  21.6 1.0 %collective-permute-done.2.outer_end = f32[216,128]{1,0:T(8,128)S(1)} collective-permute-done((f32[216,128]{1,0:T(8,128)S(1)}, f32[216,128]{1,0:T(8,128)S(1)}, u32[]{:S(2)}, u32[]{:S(2)}) %collective-permute-start.2) | collective-permute-done | bytes 110624 | tf_op jit(solution)/shard_map/ppermute | solution.py:521
  22.6 0.0 collective-permute-done.3.inner_end
  22.6 8.1 %window.1 = (f32[3,256,128]{2,1,0:T(8,128)}, f32[32,128]{1,0:T(8,128)S(1)}, f32[4,304,128]{2,1,0:T(8,128)S(1)}, f32[4,304,128]{2,1,0:T(8,128)S(1)}, f32[4,304,12...) custom-call(f32[4,304,128]{2,1,0:T(8,128)S(1)} %get-tuple-element.20, ...), custom_call_target="tpu_custom_call", output_to_operand_aliasing={{2}: (0, {}), {3}: (1, {}), {4}: (2, {}), {5}: (3, {}), {6}... | custom-call | tf_op jit(solution)/shard_map/window/pallas_call | solution.py:572
  30.7 10.6 %all_to_all.20 = f32[32,1,128]{2,1,0:T(1,128)S(1)} all-to-all(f32[32,1,128]{2,1,0:T(1,128)S(1)} %bitcast.13), channel_id=1, replica_groups=mesh['gx'=8,'gy'=4] {'gx','gy'}, dimensions={0} | all-to-all | bytes 32768 | tf_op jit(solution)/shard_map/all_to_all | solution.py:594
  41.3 0.6 %reduce_sum.9 = f32[128]{0:T(128)} reduce(f32[32,1,128]{2,1,0:T(1,128)S(1)} %all_to_all.20, f32[]{:T(128)} %constant.10.clone.1), dimensions={0,1}, to_apply=%region_0.0 | reduce | flops 3968 | bytes 16900 | tf_op jit(solution)/shard_map/reduce_sum | solution.py:595
  (1 shorter events, 0.0 us)
Async XLA Ops:
  0.6 15.0 %copy-start = (f32[3,256,128]{2,1,0:T(8,128)S(1)}, f32[3,256,128]{2,1,0:T(8,128)}, u32[]{:S(2)}) copy-start(f32[3,256,128]{2,1,0:T(8,128)} %vel_ref.3) | copy-start | bytes 1179652
  0.6 15.0 %copy-start.1 = (f32[3,256,128]{2,1,0:T(8,128)S(1)}, f32[3,256,128]{2,1,0:T(8,128)}, u32[]{:S(2)}) copy-start(f32[3,256,128]{2,1,0:T(8,128)} %seed_ref.3) | copy-start | bytes 1179652
  0.7 15.0 %copy-start.2 = (f32[3,256,128]{2,1,0:T(8,128)S(1)}, f32[3,256,128]{2,1,0:T(8,128)}, u32[]{:S(2)}) copy-start(f32[3,256,128]{2,1,0:T(8,128)} %cou_ref.3) | copy-start | bytes 1179652
  0.7 15.0 %copy-start.3 = (f32[3,256,128]{2,1,0:T(8,128)S(1)}, f32[3,256,128]{2,1,0:T(8,128)}, u32[]{:S(2)}) copy-start(f32[3,256,128]{2,1,0:T(8,128)} %vis_ref.3) | copy-start | bytes 1179652
  3.5 9.4 %collective-permute-start = (f32[320,128]{1,0:T(8,128)}, f32[320,128]{1,0:T(8,128)S(1)}, u32[]{:S(2)}, u32[]{:S(2)}) collective-permute-start(f32[320,128]{1,0:T(8,128)} %get-tuple-element.18), channel_id=1, source_target_pairs={{0,3},{1,2},{2,1},{3,0},{4,7},{5,6},{6,5},{7,4},{8,11},{9,10},{10,... | collective-permute-start | bytes 491528 | tf_op jit(solution)/shard_map/ppermute | solution.py:521
  7.5 8.2 %collective-permute-start.1 = (f32[320,128]{1,0:T(8,128)}, f32[320,128]{1,0:T(8,128)S(1)}, u32[]{:S(2)}, u32[]{:S(2)}) collective-permute-start(f32[320,128]{1,0:T(8,128)} %get-tuple-element.19), channel_id=1, source_target_pairs={{0,1},{1,0},{2,3},{3,2},{4,5},{5,4},{6,7},{7,6},{8,9},{9,8},{10,11... | collective-permute-start | bytes 491528 | tf_op jit(solution)/shard_map/ppermute | solution.py:521
  8.0 12.1 %all-to-all-start = ((f32[32,1,128]{2,1,0:T(1,128)}), f32[32,1,128]{2,1,0:T(1,128)S(1)}, u32[]{:S(2)}, u32[]{:S(2)}) async-start(f32[32,1,128]{2,1,0:T(1,128)} %bitcast.14), calls=%async_computation | async-start | bytes 32768 | tf_op jit(solution)/shard_map/all_to_all | solution.py:545
  15.7 6.9 %collective-permute-start.2 = (f32[216,128]{1,0:T(8,128)S(1)}, f32[216,128]{1,0:T(8,128)S(1)}, u32[]{:S(2)}, u32[]{:S(2)}) collective-permute-start(f32[216,128]{1,0:T(8,128)S(1)} %get-tuple-element.28), channel_id=1, source_target_pairs={{0,28},{4,8},{8,4},{12,16},{16,12},{20,24},{24,20},{28,0},{1,29},{... | collective-permute-start | bytes 331784 | tf_op jit(solution)/shard_map/ppermute | solution.py:521
  17.9 4.6 %collective-permute-start.3 = (f32[216,128]{1,0:T(8,128)S(1)}, f32[216,128]{1,0:T(8,128)S(1)}, u32[]{:S(2)}, u32[]{:S(2)}) collective-permute-start(f32[216,128]{1,0:T(8,128)S(1)} %get-tuple-element.29), channel_id=1, source_target_pairs={{0,4},{4,0},{8,12},{12,8},{16,20},{20,16},{24,28},{28,24},{1,5},{5... | collective-permute-start | bytes 331784 | tf_op jit(solution)/shard_map/ppermute | solution.py:521
